TPU v7x, 256 devices: a whole 4x4x8 slice. The times are simulated.
256 devices in a mesh: blk: 8 (over y_lo, x), grp: 32 (over z, y_hi, core).
Axes of the slice: x: 4, y: 4 (y_hi: 2, y_lo: 2; y = y_hi * 2 + y_lo), z: 8, core: 2. Of those that a mesh axis runs over, the one named last changes fastest.
Arguments:
- gate_pre: bfloat16 [4096, 2, 8192], P('blk', None, 'grp'), may hold values from -6 to 6
- up_pre: bfloat16 [4096, 2, 8192], P('blk', None, 'grp'), may hold values from -6 to 6
- first_share: float32 [4096], P('blk'), may hold values from 0.1 to 0.9
- expert_ids: int32 [4096, 2], P('blk'), may hold values from 0 to 7, all different within a row; in each aligned block of 512 rows (0 to 511, 512 to 1023, ...) at most 256 rows name the same one
- down_weight: bfloat16 [8, 8192, 6144], P('blk', 'grp'), may hold values from -0.0625 to 0.0625
Outputs:
- mixed: bfloat16 [4096, 6144], P(('blk', 'grp'))
Inputs may be any that keep to these rules, and one draw needn't show every extreme that they name: `expert_ids`: the 2 ids of a token differ. In each group's aligned block of 512 tokens no expert is named by more than 256 ids, a bound that some block reaches.
All inputs are finite; a program needn't handle non-finite values.
Results may differ from a plain program's by a relative error of at most 0.02.
Values may be sent and summed in bfloat16 or wider, within the bound.
No kernel may reach another device: no remote copies, remote signals or barrier semaphores. Data moves between devices by JAX's collectives and lax.ppermute only.
A program may use at most 192 MiB of HBM per device.

v0:
```python
import jax
import jax.numpy as jnp
from jax import lax
from jax.sharding import PartitionSpec as P


def from_behind(value, axis, by):
    size = lax.axis_size(axis)
    return lax.ppermute(value, axis, [(i, (i + by) % size) for i in range(size)])


def build_table(group_ids, experts, capacity):
    flat_ids = group_ids.reshape(-1)
    row_total = flat_ids.shape[0]
    onehot = (flat_ids[:, None] == jnp.arange(experts, dtype=jnp.int32)[None, :]).astype(jnp.int32)
    rank_rows = jnp.cumsum(onehot, axis=0) - 1
    slot_of = jnp.sum(rank_rows * onehot, axis=1)
    slot_table = jnp.full((experts, capacity), row_total, jnp.int32)
    slot_table = slot_table.at[flat_ids, slot_of].set(jnp.arange(row_total, dtype=jnp.int32))
    counts = jnp.sum(onehot, axis=0)
    return (slot_table, counts, slot_of, flat_ids)


def on_device(gate_pre, up_pre, first_share, expert_ids, down_weight):
    loop_size = lax.axis_size("blk")
    position = lax.axis_index("blk")
    group_rows = expert_ids.shape[0]
    capacity = group_rows // 2
    model_width = down_weight.shape[2]
    unit_count = gate_pre.shape[2]
    slot_weight = jnp.stack([first_share, 1.0 - first_share], axis=1)
    hidden = (
        slot_weight[:, :, None]
        * jax.nn.silu(gate_pre.astype(jnp.float32))
        * up_pre.astype(jnp.float32)
    ).astype(jnp.bfloat16)
    rows_flat = hidden.reshape(-1, unit_count)
    padded = jnp.concatenate([rows_flat, jnp.zeros((1, unit_count), jnp.bfloat16)], axis=0)
    slot_table, counts, slot_of, flat_ids = build_table(expert_ids, loop_size, capacity)

    def apply_expert(weight, expert):
        row_ids = lax.dynamic_index_in_dim(slot_table, expert, 0, keepdims=False)
        return jnp.dot(padded[row_ids], weight, preferred_element_type=jnp.float32)

    weight = down_weight[0]
    products = [apply_expert(weight, position)]
    visit_order = [position]
    moving = weight
    for hop_count in range(1, loop_size):
        moving = from_behind(moving, "blk", 1)
        expert_here = (position - hop_count) % loop_size
        products.append(apply_expert(moving, expert_here))
        visit_order.append(expert_here)
    stacked = jnp.stack(products, axis=0).reshape(loop_size * capacity, model_width)
    order_array = jnp.stack(visit_order)
    expert_range = jnp.arange(loop_size, dtype=jnp.int32)
    matches = (order_array[:, None] == expert_range[None, :]).astype(jnp.int32)
    visit_of = jnp.sum(expert_range[:, None] * matches, axis=0)
    row_visit = jnp.sum(
        (flat_ids[:, None] == expert_range[None, :]).astype(jnp.int32) * visit_of[None, :], axis=1
    )
    location = row_visit * capacity + slot_of
    partial_value = stacked[location].reshape(group_rows, 2, model_width)
    partial_value = partial_value[:, 0, :] + partial_value[:, 1, :]
    mixed = lax.psum_scatter(
        partial_value.astype(jnp.bfloat16), "grp", scatter_dimension=0, tiled=True
    )
    return mixed


def solution(mesh):
    in_specs = (
        P("blk", None, "grp"),
        P("blk", None, "grp"),
        P("blk"),
        P("blk", None),
        P("blk", "grp", None),
    )
    out_specs = P(("blk", "grp"), None)
    return jax.shard_map(
        on_device, mesh=mesh, in_specs=in_specs, out_specs=out_specs, check_vma=False
    )
```

profile of v0, /device:TPU:2, one launch (start us, length us, event | category | flops | bytes accessed | tf_op | source)
XLA Modules:
  0.0 751.9 jit_solution(855616821602069972)
XLA Ops:
  6.5 0.0 reduce-scatter.2.cloned.1.call-start
  6.5 1.5 collective-permute-start
  8.0 68.6 %collective-permute-done = bf16[256,6144]{1,0:T(8,128)(2,1)S(1)} collective-permute-done((bf16[256,6144]{1,0:T(8,128)(2,1)}, bf16[256,6144]{1,0:T(8,128)(2,1)S(1)}, u32[]{:S(2)}, u32[]{:S(2)}) %collective-permute-start) | collective-permute-done | bytes 3145760 | tf_op jit(solution)/shard_map/ppermute | solution.py:9
  76.6 1.7 copy-done
  78.3 1.5 collective-permute-start.1
  79.7 67.2 %collective-permute-done.1 = bf16[256,6144]{1,0:T(8,128)(2,1)S(1)} collective-permute-done((bf16[256,6144]{1,0:T(8,128)(2,1)S(1)}, bf16[256,6144]{1,0:T(8,128)(2,1)S(1)}, u32[]{:S(2)}, u32[]{:S(2)}) %collective-permute-start.1) | collective-permute-done | bytes 3145760 | tf_op jit(solution)/shard_map/ppermute | solution.py:9
  146.9 1.6 copy-done.2
  148.6 1.8 collective-permute-start.2
  150.4 65.7 %collective-permute-done.2 = bf16[256,6144]{1,0:T(8,128)(2,1)S(1)} collective-permute-done((bf16[256,6144]{1,0:T(8,128)(2,1)S(1)}, bf16[256,6144]{1,0:T(8,128)(2,1)S(1)}, u32[]{:S(2)}, u32[]{:S(2)}) %collective-permute-start.2) | collective-permute-done | bytes 3145760 | tf_op jit(solution)/shard_map/ppermute | solution.py:9
  216.1 1.6 copy-done.4
  217.7 2.3 collective-permute-start.3
  220.0 66.0 %collective-permute-done.3 = bf16[256,6144]{1,0:T(8,128)(2,1)S(1)} collective-permute-done((bf16[256,6144]{1,0:T(8,128)(2,1)S(1)}, bf16[256,6144]{1,0:T(8,128)(2,1)S(1)}, u32[]{:S(2)}, u32[]{:S(2)}) %collective-permute-start.3) | collective-permute-done | bytes 3145760 | tf_op jit(solution)/shard_map/ppermute | solution.py:9
  286.0 3.1 collective-permute-start.4
  289.1 0.8 copy.15
  289.9 0.2 eq.57
  290.1 0.2 eq.53
  290.3 0.2 reshape.327
  290.5 2.3 reduce-window.6
  292.8 0.3 slice_reduce_fusion
  293.1 0.2 reduce-window.9
  293.2 0.1 stack.83
  293.3 0.1 select_reduce_fusion.1
  293.4 0.1 add_bitcast_fusion
  293.5 0.1 select_reduce_fusion
  293.6 60.4 %collective-permute-done.4 = bf16[256,6144]{1,0:T(8,128)(2,1)} collective-permute-done((bf16[256,6144]{1,0:T(8,128)(2,1)S(1)}, bf16[256,6144]{1,0:T(8,128)(2,1)}, u32[]{:S(2)}, u32[]{:S(2)}) %collective-permute-start.4) | collective-permute-done | bytes 3145760 | tf_op jit(solution)/shard_map/ppermute | solution.py:9
  354.0 3.4 collective-permute-start.5
  357.4 0.7 multiply_reduce_fusion
  358.2 0.8 and_reduce_fusion
  358.9 4.5 scatter_custom_fusion
  363.5 0.7 broadcast_subtract_fusion
  364.1 0.7 pad_maximum_fusion
  364.8 0.1 copy.14
  365.0 3.4 fusion.14
  368.3 2.0 reshape.326
  370.4 0.0 copy-done.6
  370.4 1.1 concatenate.6
  371.5 1.2 gather_fusion
  372.7 1.2 gather_fusion.1
  373.8 1.2 gather_fusion.2
  375.0 1.2 gather_fusion.3
  376.2 1.2 gather_fusion.4
  377.3 1.2 gather_fusion.5
  378.5 1.2 gather_fusion.6
  379.6 1.2 gather_fusion.7
  380.8 41.1 %collective-permute-done.5 = bf16[256,6144]{1,0:T(8,128)(2,1)} collective-permute-done((bf16[256,6144]{1,0:T(8,128)(2,1)}, bf16[256,6144]{1,0:T(8,128)(2,1)}, u32[]{:S(2)}, u32[]{:S(2)}) %collective-permute-start.5) | collective-permute-done | bytes 3145760 | tf_op jit(solution)/shard_map/ppermute | solution.py:9
  421.9 3.6 collective-permute-start.6
  425.6 5.5 fusion.8
  431.1 0.0 copy-done.1
  431.1 3.7 fusion.7
  434.8 3.6 fusion.6
  438.4 0.0 copy-done.5
  438.4 3.6 fusion.5
  442.0 0.0 copy-done.7
  442.0 3.7 fusion.4
  445.7 5.6 fusion.3
  451.3 5.5 fusion.2
  456.8 31.1 %collective-permute-done.6 = bf16[256,6144]{1,0:T(8,128)(2,1)S(1)} collective-permute-done((bf16[256,6144]{1,0:T(8,128)(2,1)}, bf16[256,6144]{1,0:T(8,128)(2,1)S(1)}, u32[]{:S(2)}, u32[]{:S(2)}) %collective-permute-start.6) | collective-permute-done | bytes 3145760 | tf_op jit(solution)/shard_map/ppermute | solution.py:9
  487.9 3.6 fusion.1
  491.5 36.5 %gather_fusion.8 = f32[1024,6144]{1,0:T(8,128)} fusion(f32[2048,6144]{1,0:T(8,128)} %bitcast.121, s32[1024]{0:T(1024)S(1)} %broadcast_clamp_fusion), kind=kCustom, calls=%fused_computation.8 | custom fusion | bytes 50335744 | tf_op jit(solution)/shard_map/gather | solution.py:63
  528.0 28.0 %reshape.330 = f32[512,2,6144]{2,1,0:T(2,128)} reshape(f32[1024,6144]{1,0:T(8,128)} %gather_fusion.8) | data formatting | bytes 50331648 | tf_op jit(solution)/shard_map/reshape | solution.py:63
  556.0 29.7 %fusion.29 = (f32[512,1,6144]{2,1,0:T(1,128)S(1)}, f32[512,1,6144]{2,1,0:T(1,128)}) fusion(f32[512,2,6144]{2,1,0:T(2,128)} %reshape.330), kind=kLoop, calls=%fused_computation.93 | loop fusion | bytes 50331648 | tf_op jit(solution)/shard_map/slice | solution.py:64
  585.7 12.2 %fusion.9 = bf16[512,6144]{1,0:T(8,128)(2,1)} fusion(f32[512,1,6144]{2,1,0:T(1,128)} %get-tuple-element.8, f32[512,1,6144]{2,1,0:T(1,128)S(1)} %get-tuple-element.7), kind=kLoop, calls=%fused_computation.28 | loop fusion | flops 6291456 | bytes 31457280 | tf_op jit(solution)/shard_map/convert_element_type | solution.py:66
  597.9 0.0 reduce-scatter.2.cloned.1.call-update
  597.9 147.1 %reduce-scatter.2.cloned.1.call-done = bf16[16,6144]{1,0:T(8,128)(2,1)} async-done(((bf16[512,6144]{1,0:T(8,128)(2,1)}), bf16[16,6144]{1,0:T(8,128)(2,1)}) %reduce-scatter.2.cloned.1.call-update) | async-done | bytes 196624 | tf_op jit(solution)/shard_map/reduce_scatter | solution.py:65
  (25 shorter events, 0.1 us)
Async XLA Ops:
  6.5 738.5 %reduce-scatter.2.cloned.1.call-start = ((), (), s32[]{:S(2)}) async-start(), calls=%async_computation.1 | async-start | bytes 6488064 | tf_op jit(solution)/shard_map/reduce_scatter | solution.py:65
  6.5 70.1 %collective-permute-start = (bf16[256,6144]{1,0:T(8,128)(2,1)}, bf16[256,6144]{1,0:T(8,128)(2,1)S(1)}, u32[]{:S(2)}, u32[]{:S(2)}) collective-permute-start(bf16[256,6144]{1,0:T(8,128)(2,1)} %bitcast.122), channel_id=1, source_target_pairs={{0,32},{32,64},{64,96},{96,128},{128,160},{160,192},{192,224},{224... | collective-permute-start | bytes 9437192 | tf_op jit(solution)/shard_map/ppermute | solution.py:9
  76.6 1.7 copy-start
  78.3 68.7 %collective-permute-start.1 = (bf16[256,6144]{1,0:T(8,128)(2,1)S(1)}, bf16[256,6144]{1,0:T(8,128)(2,1)S(1)}, u32[]{:S(2)}, u32[]{:S(2)}) collective-permute-start(bf16[256,6144]{1,0:T(8,128)(2,1)S(1)} %collective-permute-done), channel_id=1, source_target_pairs={{0,32},{32,64},{64,96},{96,128},{128,160},{160,192},{192,224},{224... | collective-permute-start | bytes 9437192 | tf_op jit(solution)/shard_map/ppermute | solution.py:9
  146.9 1.6 copy-start.2
  148.6 67.5 %collective-permute-start.2 = (bf16[256,6144]{1,0:T(8,128)(2,1)S(1)}, bf16[256,6144]{1,0:T(8,128)(2,1)S(1)}, u32[]{:S(2)}, u32[]{:S(2)}) collective-permute-start(bf16[256,6144]{1,0:T(8,128)(2,1)S(1)} %collective-permute-done.1), channel_id=1, source_target_pairs={{0,32},{32,64},{64,96},{96,128},{128,160},{160,192},{192,224},{224... | collective-permute-start | bytes 9437192 | tf_op jit(solution)/shard_map/ppermute | solution.py:9
  216.1 1.6 copy-start.4
  217.7 68.3 %collective-permute-start.3 = (bf16[256,6144]{1,0:T(8,128)(2,1)S(1)}, bf16[256,6144]{1,0:T(8,128)(2,1)S(1)}, u32[]{:S(2)}, u32[]{:S(2)}) collective-permute-start(bf16[256,6144]{1,0:T(8,128)(2,1)S(1)} %collective-permute-done.2), channel_id=1, source_target_pairs={{0,32},{32,64},{64,96},{96,128},{128,160},{160,192},{192,224},{224... | collective-permute-start | bytes 9437192 | tf_op jit(solution)/shard_map/ppermute | solution.py:9
  286.0 84.4 %copy-start.6 = (bf16[256,6144]{1,0:T(8,128)(2,1)}, bf16[256,6144]{1,0:T(8,128)(2,1)S(1)}, u32[]{:S(2)}) copy-start(bf16[256,6144]{1,0:T(8,128)(2,1)S(1)} %collective-permute-done.3) | copy-start | bytes 9437188
  286.0 68.1 %collective-permute-start.4 = (bf16[256,6144]{1,0:T(8,128)(2,1)S(1)}, bf16[256,6144]{1,0:T(8,128)(2,1)}, u32[]{:S(2)}, u32[]{:S(2)}) collective-permute-start(bf16[256,6144]{1,0:T(8,128)(2,1)S(1)} %collective-permute-done.3), channel_id=1, source_target_pairs={{0,32},{32,64},{64,96},{96,128},{128,160},{160,192},{192,224},{224... | collective-permute-start | bytes 9437192 | tf_op jit(solution)/shard_map/ppermute | solution.py:9
  354.0 67.9 %collective-permute-start.5 = (bf16[256,6144]{1,0:T(8,128)(2,1)}, bf16[256,6144]{1,0:T(8,128)(2,1)}, u32[]{:S(2)}, u32[]{:S(2)}) collective-permute-start(bf16[256,6144]{1,0:T(8,128)(2,1)} %collective-permute-done.4), channel_id=1, source_target_pairs={{0,32},{32,64},{64,96},{96,128},{128,160},{160,192},{192,224},{224... | collective-permute-start | bytes 9437192 | tf_op jit(solution)/shard_map/ppermute | solution.py:9
  380.8 50.3 %copy-start.1 = (bf16[256,6144]{1,0:T(8,128)(2,1)S(1)}, bf16[256,6144]{1,0:T(8,128)(2,1)}, u32[]{:S(2)}) copy-start(bf16[256,6144]{1,0:T(8,128)(2,1)} %copy-done) | copy-start | bytes 9437188
  421.9 66.0 %collective-permute-start.6 = (bf16[256,6144]{1,0:T(8,128)(2,1)}, bf16[256,6144]{1,0:T(8,128)(2,1)S(1)}, u32[]{:S(2)}, u32[]{:S(2)}) collective-permute-start(bf16[256,6144]{1,0:T(8,128)(2,1)} %collective-permute-done.5), channel_id=1, source_target_pairs={{0,32},{32,64},{64,96},{96,128},{128,160},{160,192},{192,224},{224... | collective-permute-start | bytes 9437192 | tf_op jit(solution)/shard_map/ppermute | solution.py:9
  431.1 3.7 copy-start.3
  434.8 3.6 copy-start.5
  438.4 3.6 copy-start.7
Sparse Core Ops, SparseCore 0:
  598.0 146.9 reduce-scatter.1
where the time goes:
time: 753 us; the launch traced here: 752 us
  waiting for transfers between devices  547 us (73%)
  local copies, waits for them, and re-layouts  118 us (16%)
  matrix products  34.8 us (5%)
  other arithmetic  21.2 us (3%)
  starting transfers between devices  17.2 us (2%)
  between operations  13.7 us (2%)
    ppermute x7, waiting for transfers between devices, from_behind(): lax.ppermute(value, axis, [(i, (i + by) % size) for i in range(size)])  400 us
    reduce_scatter x1, waiting for transfers between devices, on_device(): lax.psum_scatter(partial_value.astype(jnp.bfloat16), 'grp', scatter_dimen...  147 us
    gather x1, local copies, waits for them, and re-layouts, on_device(): partial_value = stacked[location].reshape(group_rows, 2, model_width)  36.5 us
    dot_general x8, matrix products, apply_expert(): return jnp.dot(padded[row_ids], weight, preferred_element_type=jnp.float32)  34.8 us
    slice x1, local copies, waits for them, and re-layouts, on_device(): partial_value = partial_value[:, 0, :] + partial_value[:, 1, :]  29.7 us
    reshape x1, local copies, waits for them, and re-layouts, on_device(): partial_value = stacked[location].reshape(group_rows, 2, model_width)  28 us
    ppermute x7, starting transfers between devices, from_behind(): lax.ppermute(value, axis, [(i, (i + by) % size) for i in range(size)])  17.1 us
  transfers between devices with their start and end apart: 8, of which 8 were waited for; matrix products, arithmetic and copies ran while one was open for 8% of the time, Pallas kernels for 0%

commit v1 on v0

v1 whole, which is shorter than its diff:
```python
import jax
import jax.numpy as jnp
from jax import lax
from jax.experimental import pallas as pl
from jax.experimental.pallas import tpu as pltpu
from jax.sharding import PartitionSpec as P

N_CORE = 2
N_YHI = 2


def mix_kernel(ids_ref, hidden_ref, weight_ref, out_ref, wide_ref):
    experts = weight_ref.shape[0]
    units = weight_ref.shape[1]
    ids = ids_ref[0]
    first, second = hidden_ref[0, :, :units], hidden_ref[0, :, units:]
    for expert in range(experts):
        chosen = (ids == expert).astype(jnp.float32).astype(jnp.bfloat16)
        wide_ref[:, expert * units : (expert + 1) * units] = (
            first * chosen[:, 0:1] + second * chosen[:, 1:2]
        )
    weight = weight_ref[...].reshape(experts * units, weight_ref.shape[2])
    total = jnp.dot(wide_ref[...], weight, preferred_element_type=jnp.float32)
    out_ref[...] = total.astype(jnp.bfloat16).reshape(out_ref.shape)


def mix(ids, hidden, weight, out_dims):
    groups, rows, width = hidden.shape
    experts, units, columns = weight.shape
    cores, depth, keep = out_dims
    return pl.pallas_call(
        mix_kernel,
        grid=(groups,),
        in_specs=[
            pl.BlockSpec((1, rows, 2), lambda g: (g, 0, 0)),
            pl.BlockSpec((1, rows, width), lambda g: (g, 0, 0)),
            pl.BlockSpec((experts, units, columns), lambda g: (0, 0, 0)),
        ],
        out_specs=pl.BlockSpec((cores, depth, 1, keep, columns), lambda g: (0, 0, g, 0, 0)),
        out_shape=jax.ShapeDtypeStruct((cores, depth, groups, keep, columns), jnp.bfloat16),
        scratch_shapes=[pltpu.VMEM((rows, experts * units), jnp.bfloat16)],
        compiler_params=pltpu.CompilerParams(vmem_limit_bytes=48 * 1024 * 1024),
        cost_estimate=pl.CostEstimate(
            flops=2 * groups * rows * experts * units * columns,
            bytes_accessed=2 * (groups * rows * (width + columns) + experts * units * columns),
            transcendentals=0,
        ),
    )(ids, hidden, weight)


def on_device(gate_pre, up_pre, first_share, expert_ids, down_weight):
    n_blk, n_grp = lax.axis_size("blk"), lax.axis_size("grp")
    j = lax.axis_index("grp")
    core, y_hi = j % N_CORE, (j // N_CORE) % N_YHI
    n_z = n_grp // (N_CORE * N_YHI)
    rows, _, units = gate_pre.shape
    keep = rows // n_grp
    columns = down_weight.shape[2] // n_blk
    slot_weight = jnp.stack([first_share, 1.0 - first_share], axis=1)
    hidden = (
        slot_weight[:, :, None]
        * jax.nn.silu(gate_pre.astype(jnp.float32))
        * up_pre.astype(jnp.float32)
    ).astype(jnp.bfloat16)

    def mine_first(x):
        x = x.reshape((n_z * N_YHI, N_CORE, keep) + x.shape[1:])
        mine = lax.dynamic_index_in_dim(x, core, 1, keepdims=False)
        other = lax.dynamic_index_in_dim(x, 1 - core, 1, keepdims=False)
        return jnp.stack([mine, other]).reshape((rows,) + x.shape[3:])

    hidden = mine_first(hidden.reshape(rows, 2 * units))
    ids = mine_first(expert_ids)
    weight = lax.all_to_all(down_weight[0], "blk", 1, 0, tiled=True)
    weight = weight.reshape(n_blk, units, columns)
    hidden_all = lax.all_gather(hidden, "blk")
    ids_all = lax.all_gather(ids, "blk")
    partial = mix(ids_all, hidden_all, weight, (N_CORE, n_z * N_YHI, keep))

    def plus(a, b):
        return (a.astype(jnp.float32) + b.astype(jnp.float32)).astype(jnp.bfloat16)

    other_core = [(i, i ^ 1) for i in range(n_grp)]
    both = plus(partial[0], lax.ppermute(partial[1], "grp", other_core))
    along_z = [[i + z * N_CORE * N_YHI for z in range(n_z)] for i in range(N_CORE * N_YHI)]
    over_z = lax.psum_scatter(
        both, "grp", scatter_dimension=0, axis_index_groups=along_z, tiled=True
    )
    other_y = [(i, i ^ 2) for i in range(n_grp)]
    kept = lax.dynamic_index_in_dim(over_z, y_hi, 0, keepdims=False)
    sent = lax.dynamic_index_in_dim(over_z, 1 - y_hi, 0, keepdims=False)
    summed = plus(kept, lax.ppermute(sent, "grp", other_y))
    pieces = lax.all_to_all(summed, "blk", 0, 0, tiled=True)
    return jnp.swapaxes(pieces, 0, 1).reshape(keep, n_blk * columns)


def solution(mesh):
    in_specs = (
        P("blk", None, "grp"),
        P("blk", None, "grp"),
        P("blk"),
        P("blk", None),
        P("blk", "grp", None),
    )
    out_specs = P(("blk", "grp"), None)
    return jax.shard_map(
        on_device, mesh=mesh, in_specs=in_specs, out_specs=out_specs, check_vma=False
    )
```

time: 753 us -> 219 us (0.29)
  waiting for transfers between devices: 547 us -> 64.3 us
  local copies, waits for them, and re-layouts: 118 us -> 14.3 us
  blocking collectives: 0 us -> 91.7 us
  matrix products: 34.8 us -> 0 us
  Pallas kernels: 0 us -> 17.1 us
  other arithmetic: 21.2 us -> 8.54 us
  starting transfers between devices: 17.2 us -> 9.23 us
    ppermute x7 -> x2, waiting for transfers between devices: 400 us -> 9.75 us  [the longest x1 5.65 us: on_device(): both = plus(partial[0], lax.ppermute(partial[1], 'grp', other_core))]
    reduce_scatter x1, waiting for transfers between devices: 147 us -> 54.5 us  [on_device(): lax.psum_scatter(both, 'grp', scatter_dimension=0, axis_index_groups=alon...]
    all_gather x0 -> x1, blocking collectives: none -> 80.6 us  [on_device(): ids_all = lax.all_gather(ids, 'blk')]
    gather x9 -> x0, local copies, waits for them, and re-layouts: 45.7 us -> none  [the longest x1 36.5 us: on_device(): partial_value = stacked[location].reshape(group_rows, 2, model_width)]
    dot_general x8 -> x0, matrix products: 34.8 us -> none  [apply_expert(): return jnp.dot(padded[row_ids], weight, preferred_element_type=jnp.float32)]
    slice x2 -> x0, local copies, waits for them, and re-layouts: 30 us -> none  [the longest x1 29.7 us: on_device(): partial_value = partial_value[:, 0, :] + partial_value[:, 1, :]]
    reshape x3 -> x2, local copies, waits for them, and re-layouts: 30.2 us -> 0.79 us  [the longest x1 0.69 us: on_device(): return jnp.swapaxes(pieces, 0, 1).reshape(keep, n_blk * columns)]
    pallas_call x0 -> x1, Pallas kernels: none -> 17.1 us  [mix(): pl.pallas_call(mix_kernel, grid=(groups,), in_specs=[pl.BlockSpec((1, row...]
  transfers between devices with their start and end apart: 8 -> 5, of which waited for: 8 -> 3; matrix products, arithmetic and copies ran while one was open for 8% -> 4% of each run, Pallas kernels for 0% -> 0%
where the time goes in v1:
time: 219 us
  blocking collectives  91.7 us (42%)
  waiting for transfers between devices  64.3 us (29%)
  Pallas kernels  17.1 us (8%)
  local copies, waits for them, and re-layouts  14.3 us (7%)
  between operations  13.5 us (6%)
  starting transfers between devices  9.23 us (4%)
  other arithmetic  8.54 us (4%)
    all_gather x1, blocking collectives, on_device(): ids_all = lax.all_gather(ids, 'blk')  80.6 us
    reduce_scatter x1, waiting for transfers between devices, on_device(): lax.psum_scatter(both, 'grp', scatter_dimension=0, axis_index_groups=alon...  54.5 us
    pallas_call x1, Pallas kernels, mix(): pl.pallas_call(mix_kernel, grid=(groups,), in_specs=[pl.BlockSpec((1, row...  17.1 us
    all_to_all x1, blocking collectives, on_device(): pieces = lax.all_to_all(summed, 'blk', 0, 0, tiled=True)  11.1 us
    all_to_all x1, starting transfers between devices, on_device(): weight = lax.all_to_all(down_weight[0], 'blk', 1, 0, tiled=True)  5.97 us
    ppermute x1, waiting for transfers between devices, on_device(): both = plus(partial[0], lax.ppermute(partial[1], 'grp', other_core))  5.65 us
    unnamed x7, local copies, waits for them, and re-layouts  4.77 us
  transfers between devices with their start and end apart: 5, of which 3 were waited for; matrix products, arithmetic and copies ran while one was open for 4% of the time, Pallas kernels for 0%

profile of v1, /device:TPU:2, one launch (start us, length us, event | category | flops | bytes accessed | tf_op | source)
XLA Modules:
  0.0 218.8 jit_solution(16659803600454900177)
XLA Ops:
  6.5 0.0 all-gather.2.cloned.1.call-start
  6.5 0.7 broadcast_subtract_fusion
  7.2 0.7 pad_maximum_fusion.1
  7.9 0.1 copy.17
  8.1 2.7 %fusion.5 = bf16[512,2,256]{2,1,0:T(2,128)(2,1)S(1)} fusion(bf16[512,2,256]{2,1,0:T(2,128)(2,1)} %param.6, bf16[512,2,256]{2,1,0:T(2,128)(2,1)} %param.5, f32[512,2]{1,0:T(8,128)S(1)} %copy.17), kind=kLoop, calls=%fused_computation.10 | loop fusion | flops 2359296 | bytes 1576960 | tf_op jit(solution)/shard_map/convert_element_type | solution.py:64
  10.7 0.3 reshape_reshape.3
  11.1 0.9 pad_maximum_fusion
  12.0 0.0 all-gather.2.cloned.1.call-update
  12.0 3.2 %copy.18 = bf16[1,256,6144]{1,2,0:T(8,128)(2,1)S(1)} copy(bf16[1,256,6144]{2,1,0:T(8,128)(2,1)} %param.9) | data formatting | bytes 6291456 | tf_op args[4]
  15.2 2.8 %copy.19 = bf16[256,8,768]{2,0,1:T(8,128)(2,1)} copy(bf16[256,8,768]{0,2,1:T(8,128)(2,1)S(1)} %bitcast.37) | data formatting | bytes 6291456 | tf_op jit(solution)/shard_map/all_to_all | solution.py:74
  18.0 0.0 copy-start.2
  18.0 6.0 %all-to-all-start = ((bf16[256,8,768]{2,0,1:T(8,128)(2,1)}), bf16[256,8,768]{2,0,1:T(8,128)(2,1)S(1)}, u32[]{:S(2)}, u32[]{:S(2)}) async-start(bf16[256,8,768]{2,0,1:T(8,128)(2,1)} %copy.19), calls=%async_computation | async-start | bytes 6291456 | tf_op jit(solution)/shard_map/all_to_all | solution.py:74
  24.0 0.0 reduce-scatter.2.cloned.1.call-start
  24.0 0.0 copy-done.2
  24.0 0.1 reshape.21
  24.2 0.1 all_gather_reshape.6
  24.3 80.6 %all_gather.6 = s32[8,512,2]{1,2,0:T(2,128)S(1)} all-gather(s32[1,512,2]{1,2,0:T(2,128)S(1)} %all_gather_reshape.6), channel_id=1, replica_groups=mesh['blk'=8,'grp'=32] {'blk'}, dimensions={0}, use_global_device_ids=true | all-gather | bytes 36864 | tf_op jit(solution)/shard_map/all_gather | solution.py:77
  104.9 2.0 copy.20.ids_ref
  106.9 0.0 all-to-all-done
  106.9 0.0 all-gather.2.cloned.1.call-done.hidden_ref
  106.9 0.0 copy-start
  106.9 1.6 copy-done
  108.5 17.1 %shard_map.55 = bf16[2,16,8,16,768]{4,3,2,1,0:T(8,128)(2,1)} custom-call(s32[8,512,2]{2,1,0:T(8,128)S(1)} %copy-done, bf16[8,512,512]{2,1,0:T(8,128)(2,1)} %all-gather.2.cloned.1.call-done.hidden_ref, bf16[8,256,768]{2,1,0:T(8,128)(2,1)S(1)} %bitcast.36), custom_call_target="tpu_custom_call" | custom-call | flops 12884901888 | bytes 13631488 | tf_op jit(solution)/shard_map/pallas_call | solution.py:31
  125.6 0.0 copy-start.1
  125.6 2.3 %slice_bitcast_fusion = bf16[16,8,16,768]{3,2,1,0:T(8,128)(2,1)S(1)} fusion(bf16[2,16,8,16,768]{4,3,2,1,0:T(8,128)(2,1)} %shard_map.55), kind=kLoop, calls=%fused_computation.2 | loop fusion | bytes 6291456 | tf_op jit(solution)/shard_map/squeeze | solution.py:84
  128.0 0.1 collective-permute-start
  128.1 5.6 %collective-permute-done = bf16[16,8,16,768]{3,2,1,0:T(8,128)(2,1)S(1)} collective-permute-done((bf16[16,8,16,768]{3,2,1,0:T(8,128)(2,1)S(1)}, bf16[16,8,16,768]{3,2,1,0:T(8,128)(2,1)S(1)}, u32[]{:S(2)}, u32[]{:S(2)}) %collective-permute-start) | collective-permute-done | bytes 3145760 | tf_op jit(solution)/shard_map/ppermute | solution.py:84
  133.7 0.0 copy-done.1
  133.7 2.6 %fusion = bf16[16,8,16,768]{3,2,1,0:T(8,128)(2,1)} fusion(bf16[16,8,16,768]{3,2,1,0:T(8,128)(2,1)S(1)} %collective-permute-done, bf16[2,16,8,16,768]{4,3,2,1,0:T(8,128)(2,1)S(1)} %copy-done.1), kind=kLoop, calls=%fused_computation.1 | loop fusion | flops 6291456 | bytes 9437184 | tf_op jit(solution)/shard_map/convert_element_type | solution.py:81
  136.4 0.0 reduce-scatter.2.cloned.1.call-update
  136.4 54.5 %reduce-scatter.2.cloned.1.call-done = bf16[2,8,16,768]{3,2,1,0:T(8,128)(2,1)} async-done(((bf16[16,8,16,768]{3,2,1,0:T(8,128)(2,1)}), bf16[2,8,16,768]{3,2,1,0:T(8,128)(2,1)}) %reduce-scatter.2.cloned.1.call-update) | async-done | bytes 393232 | tf_op jit(solution)/shard_map/reduce_scatter | solution.py:86
  190.9 0.9 dynamic-slice_bitcast_fusion.2
  191.8 3.2 %collective-permute-start.1 = (bf16[8,16,768]{2,1,0:T(8,128)(2,1)S(1)}, bf16[8,16,768]{2,1,0:T(8,128)(2,1)S(1)}, u32[]{:S(2)}, u32[]{:S(2)}) collective-permute-start(bf16[8,16,768]{2,1,0:T(8,128)(2,1)S(1)} %dynamic-slice_bitcast_fusion.2), channel_id=1, source_target_pairs={{0,2},{1,3},{2,0},{3,1},{4,6},{5,7},{6,4},{7,5},{8,10},{9,11},{10,... | collective-permute-start | bytes 589832 | tf_op jit(solution)/shard_map/ppermute | solution.py:92
  195.0 4.1 %collective-permute-done.1 = bf16[8,16,768]{2,1,0:T(8,128)(2,1)S(1)} collective-permute-done((bf16[8,16,768]{2,1,0:T(8,128)(2,1)S(1)}, bf16[8,16,768]{2,1,0:T(8,128)(2,1)S(1)}, u32[]{:S(2)}, u32[]{:S(2)}) %collective-permute-start.1) | collective-permute-done | bytes 196640 | tf_op jit(solution)/shard_map/ppermute | solution.py:92
  199.1 1.0 fusion.6
  200.1 11.1 %all_to_all.21 = bf16[8,16,768]{2,1,0:T(8,128)(2,1)S(1)} all-to-all(bf16[8,16,768]{2,1,0:T(8,128)(2,1)S(1)} %fusion.6), channel_id=1, replica_groups=mesh['blk'=8,'grp'=32] {'blk'}, dimensions={0} | all-to-all | bytes 393216 | tf_op jit(solution)/shard_map/all_to_all | solution.py:93
  211.2 0.7 copy.24
  (4 shorter events, 0.1 us)
Async XLA Ops:
  6.5 100.4 %all-gather.2.cloned.1.call-start = ((), (), s32[]{:S(2)}) async-start(), calls=%async_computation.3 | async-start | bytes 4718592 | tf_op jit(solution)/shard_map/all_gather | solution.py:76
  18.0 6.0 %copy-start.2 = (s32[512,2]{0,1:T(2,128)S(1)}, s32[512,2]{0,1:T(2,128)}, u32[]{:S(2)}) copy-start(s32[512,2]{0,1:T(2,128)} %param.8) | copy-start | bytes 12292
  18.0 88.9 %all-to-all-start = ((bf16[256,8,768]{2,0,1:T(8,128)(2,1)}), bf16[256,8,768]{2,0,1:T(8,128)(2,1)S(1)}, u32[]{:S(2)}, u32[]{:S(2)}) async-start(bf16[256,8,768]{2,0,1:T(8,128)(2,1)} %copy.19), calls=%async_computation | async-start | bytes 6291456 | tf_op jit(solution)/shard_map/all_to_all | solution.py:74
  24.0 166.9 %reduce-scatter.2.cloned.1.call-start = ((), (), s32[]{:S(2)}) async-start(), calls=%async_computation.4 | async-start | bytes 3538944 | tf_op jit(solution)/shard_map/reduce_scatter | solution.py:86
  106.9 1.6 copy-start
  125.6 8.1 %copy-start.1 = (bf16[2,16,8,16,768]{4,3,2,1,0:T(8,128)(2,1)S(1)}, bf16[2,16,8,16,768]{4,3,2,1,0:T(8,128)(2,1)}, u32[]{:S(2)}) copy-start(bf16[2,16,8,16,768]{4,3,2,1,0:T(8,128)(2,1)} %shard_map.55) | copy-start | bytes 18874372
  128.0 5.7 %collective-permute-start = (bf16[16,8,16,768]{3,2,1,0:T(8,128)(2,1)S(1)}, bf16[16,8,16,768]{3,2,1,0:T(8,128)(2,1)S(1)}, u32[]{:S(2)}, u32[]{:S(2)}) collective-permute-start(bf16[16,8,16,768]{3,2,1,0:T(8,128)(2,1)S(1)} %slice_bitcast_fusion), channel_id=1, source_target_pairs={{0,1},{1,0},{2,3},{3,2},{4,5},{5,4},{6,7},{7,6},{8,9},{9,8},{10,11... | collective-permute-start | bytes 9437192 | tf_op jit(solution)/shard_map/ppermute | solution.py:84
  191.8 7.3 %collective-permute-start.1 = (bf16[8,16,768]{2,1,0:T(8,128)(2,1)S(1)}, bf16[8,16,768]{2,1,0:T(8,128)(2,1)S(1)}, u32[]{:S(2)}, u32[]{:S(2)}) collective-permute-start(bf16[8,16,768]{2,1,0:T(8,128)(2,1)S(1)} %dynamic-slice_bitcast_fusion.2), channel_id=1, source_target_pairs={{0,2},{1,3},{2,0},{3,1},{4,6},{5,7},{6,4},{7,5},{8,10},{9,11},{10,... | collective-permute-start | bytes 589832 | tf_op jit(solution)/shard_map/ppermute | solution.py:92
Sparse Core Ops, SparseCore 0:
  12.2 94.5 all-gather.1
  136.5 54.3 reduce-scatter.1

commit v2 on v0

v2 whole, which is shorter than its diff:
```python
import jax
import jax.numpy as jnp
from jax import lax
from jax.experimental import pallas as pl
from jax.experimental.pallas import tpu as pltpu
from jax.sharding import Mesh, PartitionSpec as P

ID_ROWS = 16
LONG = 10**12
LIMIT = 56 * 1024 * 1024
HBM = pl.BlockSpec(memory_space=pl.ANY)
SMEM = pl.BlockSpec(memory_space=pltpu.SMEM)
VMEM = pl.BlockSpec(memory_space=pltpu.VMEM)


def mix_kernel(count, experts, turned, place_ref, *refs):
    messages, weights = refs[:count], refs[count : count + experts]
    mine_ref, other_ref, weight_ref, message_ref, wide_ref, got_weight, got_message = refs[
        count + experts :
    ]
    rows = wide_ref.shape[1]
    units = weight_ref.shape[0] // experts
    depth, keep = mine_ref.shape[0], mine_ref.shape[2]
    columns = weight_ref.shape[1]
    copies = [
        pltpu.make_async_copy(message, message_ref.at[i], got_message.at[i])
        for i, message in enumerate(messages)
    ]
    loads = [
        pltpu.make_async_copy(
            weight, weight_ref.at[pl.ds(e * units, units)], got_weight.at[e]
        )
        for e, weight in enumerate(weights)
    ]
    for load in copies + loads:
        load.start()
    is_odd = place_ref[0] == 1
    for load in copies + loads:
        load.wait()
    for i in range(count):
        ids = jnp.transpose(message_ref[i, rows:, :].astype(jnp.float32))
        first, second = message_ref[i, :rows, :units], message_ref[i, :rows, units:]
        for e in range(experts):
            expert = place_ref[2 + e].astype(jnp.float32)
            chosen = (ids == expert).astype(jnp.float32).astype(jnp.bfloat16)
            wide_ref[i % 2, :, e * units : (e + 1) * units] = (
                first * chosen[:, 0:1] + second * chosen[:, 1:2]
            )
        total = jnp.dot(wide_ref[i % 2], weight_ref[...], preferred_element_type=jnp.float32)
        total = total.astype(jnp.bfloat16).reshape(depth, 2, keep, columns)
        even, odd = total[:, 0], total[:, 1]
        mine, other = jnp.where(is_odd, odd, even), jnp.where(is_odd, even, odd)
        if not turned:
            mine_ref[:, i] = mine
            other_ref[:, i] = other
            continue
        for z in range(depth // 2):
            at = (z - place_ref[1] + depth // 2) % (depth // 2) * 2
            mine_ref[pl.ds(at, 2), i] = mine[2 * z : 2 * z + 2]
            other_ref[pl.ds(at, 2), i] = other[2 * z : 2 * z + 2]


def mix(messages, weights, place, depth, turned):
    count, experts = len(messages), len(weights)
    rows, width = messages[0].shape
    rows -= ID_ROWS
    units, columns = weights[0].shape
    keep = rows // depth // 2
    shape = jax.ShapeDtypeStruct((depth, count, keep, columns), jnp.bfloat16)
    return pl.pallas_call(
        lambda *refs: mix_kernel(count, experts, turned, *refs),
        in_specs=[SMEM] + [HBM] * (count + experts),
        out_specs=[VMEM, VMEM],
        out_shape=[shape, shape],
        scratch_shapes=[
            pltpu.VMEM((experts * units, columns), jnp.bfloat16),
            pltpu.VMEM((count, rows + ID_ROWS, width), jnp.bfloat16),
            pltpu.VMEM((2, rows, experts * units), jnp.bfloat16),
            pltpu.SemaphoreType.DMA((experts,)),
            pltpu.SemaphoreType.DMA((count,)),
        ],
        compiler_params=pltpu.CompilerParams(vmem_limit_bytes=LIMIT),
        cost_estimate=pl.CostEstimate(flops=LONG, bytes_accessed=1000, transcendentals=0),
    )(place, *messages, *weights)


def cut_kernel(order_ref, x_ref, *refs):
    outs, sem = refs[:-1], refs[-1]
    columns = outs[0].shape[1]
    copies = [
        pltpu.make_async_copy(
            x_ref.at[:, pl.ds(pl.multiple_of(order_ref[p] * columns, columns), columns)],
            out,
            sem.at[p],
        )
        for p, out in enumerate(outs)
    ]
    for copy in copies:
        copy.start()
    for copy in copies:
        copy.wait()


def cut(x, order):
    parts = order.shape[0]
    rows, columns = x.shape
    shape = jax.ShapeDtypeStruct((rows, columns // parts), x.dtype)
    return pl.pallas_call(
        cut_kernel,
        in_specs=[SMEM, VMEM],
        out_specs=[HBM] * parts,
        out_shape=[shape] * parts,
        scratch_shapes=[pltpu.SemaphoreType.DMA((parts,))],
        compiler_params=pltpu.CompilerParams(vmem_limit_bytes=LIMIT),
        cost_estimate=pl.CostEstimate(
            flops=0, bytes_accessed=4 * rows * columns, transcendentals=0
        ),
    )(order, x)


def wide_sum(*terms):
    return sum(t.astype(jnp.float32) for t in terms).astype(jnp.bfloat16)


def shift(value, axis, by):
    size = lax.axis_size(axis)
    return lax.ppermute(value, axis, [(i, (i + by) % size) for i in range(size)])


def on_device(gate_pre, up_pre, first_share, expert_ids, down_weight):
    n_x, n_z, n_y = lax.axis_size("x"), lax.axis_size("z"), lax.axis_size("y_hi")
    x, y, z = (lax.axis_index(a).astype(jnp.int32) for a in ("x", "y_lo", "z"))
    core = lax.axis_index("core").astype(jnp.int32)
    rows, _, units = gate_pre.shape
    columns = down_weight.shape[2] // (2 * n_x)
    depth = n_z * n_y
    keep = rows // depth // 2
    slot_weight = jnp.stack([first_share, 1.0 - first_share], axis=1)
    hidden = (
        slot_weight[:, :, None]
        * jax.nn.silu(gate_pre.astype(jnp.float32))
        * up_pre.astype(jnp.float32)
    ).astype(jnp.bfloat16)
    id_rows = jnp.pad(expert_ids.T.astype(jnp.bfloat16), ((0, ID_ROWS - 2), (0, 0)))
    here = jnp.concatenate([hidden.reshape(rows, 2 * units), id_rows], axis=0)

    across = shift(here, "y_lo", 1)
    left, right, far = shift(here, "x", 1), shift(here, "x", -1), shift(here, "x", 2)
    left_across, right_across = shift(across, "x", 1), shift(across, "x", -1)
    far_across = shift(far, "y_lo", 1)

    steps = [(dy, dx) for dx in (0, 2, 1, 3) for dy in (0, 1)]
    to = jnp.stack([(y + dy) % 2 * n_x + (x + dx) % n_x for dy, dx in steps])
    source = [(y + dy) % 2 * n_x + (x - dx) % n_x for dy, dx in steps]
    weights = list(cut(down_weight[0], to))
    for i, (dy, dx) in enumerate(steps):
        if i:
            pairs = [
                (b, (b // n_x + dy) % 2 * n_x + (b + dx) % n_x) for b in range(2 * n_x)
            ]
            weights[i] = lax.ppermute(weights[i], ("y_lo", "x"), pairs)

    place = jnp.stack([core, z] + source)

    def both_cores(messages, turned):
        mine, other = mix(messages, weights, place, depth, turned)
        return mine, lax.ppermute(other, "core", [(0, 1), (1, 0)])

    most = wide_sum(*both_cores([here, across, right, left], False))
    most = lax.psum_scatter(most, "z", scatter_dimension=0, tiled=True)
    rest = both_cores([left_across, right_across, far_across, far], True)

    def terms(by):
        return [r[n_y * by : n_y * (by + 1)] for r in rest]

    half = n_z // 2
    up = wide_sum(*terms(half))
    for by in range(half - 1, 0, -1):
        up = wide_sum(shift(up, "z", 1), *terms(by))
    down = wide_sum(*terms(half + 1))
    for by in range(half + 2, n_z):
        down = wide_sum(shift(down, "z", -1), *terms(by))
    rest = wide_sum(shift(up, "z", 1), shift(down, "z", -1), *terms(0))

    by_place = jnp.stack(
        [
            jnp.stack([most[:, 0], most[:, 2], rest[:, 3], most[:, 3]], axis=1),
            jnp.stack([most[:, 1], rest[:, 1], rest[:, 2], rest[:, 0]], axis=1),
        ],
        axis=1,
    )
    by_place = jnp.where(y == 1, by_place[:, ::-1], by_place)
    by_place = lax.dynamic_slice_in_dim(
        jnp.concatenate([by_place, by_place], axis=2), (n_x - x) % n_x, n_x, axis=2
    )
    pieces = by_place.reshape(n_y * 2 * n_x, keep, columns)
    pieces = lax.all_to_all(pieces, ("y_hi", "y_lo", "x"), 0, 0, tiled=True)
    pieces = pieces.reshape(n_y, 2 * n_x, keep, columns)
    total = wide_sum(pieces[0], pieces[1])
    return jnp.swapaxes(total, 0, 1).reshape(keep, 2 * n_x * columns)


def solution(mesh):
    names = ("y_lo", "x", "z", "y_hi", "core")
    split = Mesh(mesh.devices.reshape(2, mesh.shape["blk"] // 2, mesh.shape["grp"] // 4, 2, 2), names)
    blk, grp = names[:2], names[2:]
    in_specs = (P(blk, None, grp), P(blk, None, grp), P(blk), P(blk, None), P(blk, grp, None))
    return jax.shard_map(
        on_device, mesh=split, in_specs=in_specs, out_specs=P(names, None), check_vma=False
    )
```

time: 753 us -> 176 us (0.23)
  waiting for transfers between devices: 547 us -> 75.2 us
  local copies, waits for them, and re-layouts: 118 us -> 5.38 us
  matrix products: 34.8 us -> 0 us
  Pallas kernels: 0 us -> 27.8 us
  blocking collectives: 0 us -> 15.3 us
  starting transfers between devices: 17.2 us -> 31.9 us
  other arithmetic: 21.2 us -> 6.73 us
    ppermute x7 -> x23, waiting for transfers between devices: 400 us -> 75.2 us  [the longest x7 43.4 us: on_device(): weights[i] = lax.ppermute(weights[i], ('y_lo', 'x'), pairs)]
    reduce_scatter x1, waiting for transfers between devices: 147 us -> 0.02 us  [on_device(): most = lax.psum_scatter(most, 'z', scatter_dimension=0, tiled=True)]
    gather x9 -> x0, local copies, waits for them, and re-layouts: 45.7 us -> none  [the longest x1 36.5 us: on_device(): partial_value = stacked[location].reshape(group_rows, 2, model_width)]
    dot_general x8 -> x0, matrix products: 34.8 us -> none  [apply_expert(): return jnp.dot(padded[row_ids], weight, preferred_element_type=jnp.float32)]
    reshape x3 -> x1, local copies, waits for them, and re-layouts: 30.2 us -> 0.69 us  [on_device(): return jnp.swapaxes(total, 0, 1).reshape(keep, 2 * n_x * columns)]
    slice x2 -> x3, local copies, waits for them, and re-layouts: 30 us -> 0.91 us  [the longest x1 0.89 us: on_device(): most[:, 0]]
    pallas_call x0 -> x3, Pallas kernels: none -> 27.8 us  [the longest x2 24.1 us: mix(): pl.pallas_call(lambda *refs: mix_kernel(count, experts, turned, *refs), i...]
    all_to_all x0 -> x1, blocking collectives: none -> 15.3 us  [on_device(): pieces = lax.all_to_all(pieces, ('y_hi', 'y_lo', 'x'), 0, 0, tiled=True)]
  transfers between devices with their start and end apart: 8 -> 24, of which waited for: 8 -> 13; matrix products, arithmetic and copies ran while one was open for 8% -> 4% of each run, Pallas kernels for 0% -> 14%
where the time goes in v2:
time: 176 us
  waiting for transfers between devices  75.2 us (43%)
  starting transfers between devices  31.9 us (18%)
  Pallas kernels  27.8 us (16%)
  blocking collectives  15.3 us (9%)
  between operations  13.7 us (8%)
  other arithmetic  6.73 us (4%)
  local copies, waits for them, and re-layouts  5.38 us (3%)
    ppermute x7, waiting for transfers between devices, on_device(): weights[i] = lax.ppermute(weights[i], ('y_lo', 'x'), pairs)  43.4 us
    ppermute x14, waiting for transfers between devices, shift(): lax.ppermute(value, axis, [(i, (i + by) % size) for i in range(size)])  31.7 us
    pallas_call x2, Pallas kernels, mix(): pl.pallas_call(lambda *refs: mix_kernel(count, experts, turned, *refs), i...  24.1 us
    ppermute x14, starting transfers between devices, shift(): lax.ppermute(value, axis, [(i, (i + by) % size) for i in range(size)])  19.7 us
    all_to_all x1, blocking collectives, on_device(): pieces = lax.all_to_all(pieces, ('y_hi', 'y_lo', 'x'), 0, 0, tiled=True)  15.3 us
    ppermute x7, starting transfers between devices, on_device(): weights[i] = lax.ppermute(weights[i], ('y_lo', 'x'), pairs)  11.3 us
    convert_element_type x6, other arithmetic, wide_sum(): return sum((t.astype(jnp.float32) for t in terms)).astype(jnp.bfloat16)  4.67 us
    pallas_call x1, Pallas kernels, cut(): pl.pallas_call(cut_kernel, in_specs=[SMEM, VMEM], out_specs=[HBM] * parts...  3.77 us
  transfers between devices with their start and end apart: 24, of which 13 were waited for; matrix products, arithmetic and copies ran while one was open for 4% of the time, Pallas kernels for 14%

profile of v2, /device:TPU:2, one launch (start us, length us, event | category | flops | bytes accessed | tf_op | source)
XLA Modules:
  0.0 176.1 jit_solution(13632438389630417276)
XLA Ops:
  6.5 0.6 stack.101.order_ref
  7.2 3.8 %shard_map.55 = (bf16[256,768]{1,0:T(8,128)(2,1)}, bf16[256,768]{1,0:T(8,128)(2,1)}, bf16[256,768]{1,0:T(8,128)(2,1)}, bf16[256,768]{1,0:T(8,128)(2,1)}, bf16[25...) custom-call(s32[8]{0:T(128)} %stack.101.order_ref, ...), custom_call_target="tpu_custom_call" | custom-call | bytes 6291456 | tf_op jit(solution)/shard_map/pallas_call | solution.py:108
  11.0 1.7 collective-permute-start.3
  12.6 2.1 %collective-permute-start.4 = (bf16[256,768]{1,0:T(8,128)(2,1)}, bf16[256,768]{1,0:T(8,128)(2,1)S(1)}, u32[]{:S(2)}, u32[]{:S(2)}) collective-permute-start(bf16[256,768]{1,0:T(8,128)(2,1)} %get-tuple-element.19), channel_id=1, source_target_pairs={{0,64},{32,96},{64,0},{96,32},{128,192},{160,224},{192,128},{224,1... | collective-permute-start | bytes 1179656 | tf_op jit(solution)/shard_map/ppermute | solution.py:161
  14.7 1.3 collective-permute-start.5
  16.0 1.5 collective-permute-start.6
  17.5 2.2 %collective-permute-start.7 = (bf16[256,768]{1,0:T(8,128)(2,1)}, bf16[256,768]{1,0:T(8,128)(2,1)}, u32[]{:S(2)}, u32[]{:S(2)}) collective-permute-start(bf16[256,768]{1,0:T(8,128)(2,1)} %get-tuple-element.22), channel_id=1, source_target_pairs={{0,160},{32,192},{64,224},{96,128},{128,32},{160,64},{192,96},{224... | collective-permute-start | bytes 1179656 | tf_op jit(solution)/shard_map/ppermute | solution.py:161
  19.8 0.0 copy-start.6
  19.8 0.1 copy.8
  19.9 1.6 fusion.5
  21.6 0.1 copy.12
  21.7 0.4 collective-permute-done.3.refs_6_
  22.1 0.8 collective-permute-start.8
  22.9 3.5 %collective-permute-done.4.refs_7_ = bf16[256,768]{1,0:T(8,128)(2,1)S(1)} collective-permute-done((bf16[256,768]{1,0:T(8,128)(2,1)}, bf16[256,768]{1,0:T(8,128)(2,1)S(1)}, u32[]{:S(2)}, u32[]{:S(2)}) %collective-permute-start.4) | collective-permute-done | bytes 393248 | tf_op jit(solution)/shard_map/ppermute | solution.py:161
  26.5 0.4 collective-permute-start
  26.9 7.9 %collective-permute-done.5.refs_8_ = bf16[256,768]{1,0:T(8,128)(2,1)S(1)} collective-permute-done((bf16[256,768]{1,0:T(8,128)(2,1)}, bf16[256,768]{1,0:T(8,128)(2,1)S(1)}, u32[]{:S(2)}, u32[]{:S(2)}) %collective-permute-start.5) | collective-permute-done | bytes 393248 | tf_op jit(solution)/shard_map/ppermute | solution.py:161
  34.8 2.1 %collective-permute-start.13 = (bf16[528,512]{1,0:T(8,128)(2,1)S(1)}, bf16[528,512]{1,0:T(8,128)(2,1)}, u32[]{:S(2)}, u32[]{:S(2)}) collective-permute-start(bf16[528,512]{1,0:T(8,128)(2,1)S(1)} %fusion.6.refs_1_), channel_id=1, source_target_pairs={{0,64},{32,96},{64,0},{96,32},{1,65},{33,97},{65,1},{97,33},{2,66}... | collective-permute-start | bytes 1622024 | tf_op jit(solution)/shard_map/ppermute | solution.py:127
  36.9 6.5 %collective-permute-done.6.refs_9_ = bf16[256,768]{1,0:T(8,128)(2,1)S(1)} collective-permute-done((bf16[256,768]{1,0:T(8,128)(2,1)}, bf16[256,768]{1,0:T(8,128)(2,1)S(1)}, u32[]{:S(2)}, u32[]{:S(2)}) %collective-permute-start.6) | collective-permute-done | bytes 393248 | tf_op jit(solution)/shard_map/ppermute | solution.py:161
  43.3 0.0 collective-permute-start.1
  43.3 8.5 %collective-permute-done.7.refs_10_ = bf16[256,768]{1,0:T(8,128)(2,1)} collective-permute-done((bf16[256,768]{1,0:T(8,128)(2,1)}, bf16[256,768]{1,0:T(8,128)(2,1)}, u32[]{:S(2)}, u32[]{:S(2)}) %collective-permute-start.7) | collective-permute-done | bytes 393248 | tf_op jit(solution)/shard_map/ppermute | solution.py:161
  51.8 1.3 collective-permute-start.2
  53.1 0.0 collective-permute-done.8.refs_11_
  53.1 1.8 collective-permute-start.9
  54.8 0.7 stack.91.refs_0_
  55.5 1.3 collective-permute-start.11
  56.8 16.6 %collective-permute-done.9.refs_12_ = bf16[256,768]{1,0:T(8,128)(2,1)} collective-permute-done((bf16[256,768]{1,0:T(8,128)(2,1)}, bf16[256,768]{1,0:T(8,128)(2,1)}, u32[]{:S(2)}, u32[]{:S(2)}) %collective-permute-start.9) | collective-permute-done | bytes 393248 | tf_op jit(solution)/shard_map/ppermute | solution.py:161
  73.4 0.6 collective-permute-start.12
  74.1 0.0 collective-permute-done.13.refs_4_
  74.1 1.6 collective-permute-start.14
  75.7 0.0 collective-permute-done.1.refs_3_
  75.7 0.0 collective-permute-done.2.refs_4_
  75.8 0.7 copy-done.7
  76.5 0.2 copy-done.8
  76.7 11.9 %shard_map.56 = (bf16[16,4,16,768]{3,2,1,0:T(8,128)(2,1)}, bf16[16,4,16,768]{3,2,1,0:T(8,128)(2,1)}) custom-call(s32[10]{0:T(128)} %stack.91.refs_0_, bf16[528,512]{1,0:T(8,128)(2,1)} %copy-done.2, bf16[528,512]{1,0:T(8,128)(2,1)} %collective-permute-done.refs_2_, bf16[528,512]{1,0:T(8,128)(2,1)} %copy-done.7, bf16[528,512]{1,0:T(8,128)(2,1)} %copy-done.8, ...), custom_call_target="tpu_custom_call" | custom-call | flops 999999995904 | bytes 1000 | tf_op jit(solution)/shard_map/pallas_call | solution.py:70
  88.6 0.3 collective-permute-start.10
  89.0 12.1 %shard_map.57 = (bf16[16,4,16,768]{3,2,1,0:T(8,128)(2,1)}, bf16[16,4,16,768]{3,2,1,0:T(8,128)(2,1)}) custom-call(s32[10]{0:T(128)} %stack.91.refs_0_, bf16[528,512]{1,0:T(8,128)(2,1)} %collective-permute-done.11.refs_1_, bf16[528,512]{1,0:T(8,128)(2,1)} %collective-permute-done.12.refs_2_, bf16[528,512]{1,0:T(8,128)(2,1)} %collective-permute-done.14.refs_3_, ...), custom_call_target="tpu_custom_call" | custom-call | flops 999999995904 | bytes 1000 | tf_op jit(solution)/shard_map/pallas_call | solution.py:70
  101.1 0.6 collective-permute-start.15
  101.7 3.1 %add_convert_fusion = bf16[16,4,16,768]{3,2,1,0:T(8,128)(2,1)} fusion(bf16[16,4,16,768]{3,2,1,0:T(8,128)(2,1)} %collective-permute-done.10, bf16[16,4,16,768]{3,2,1,0:T(8,128)(2,1)S(1)} %copy-done), kind=kLoop, calls=%fused_computation | loop fusion | flops 3145728 | bytes 4718592 | tf_op jit(solution)/shard_map/convert_element_type | solution.py:122
  104.8 0.0 reduce-scatter.2.cloned.1.call-update
  104.8 0.1 collective-permute-done.15
  104.9 1.2 copy-done.1
  106.2 2.0 %collective-permute-start.16 = (bf16[2,4,16,768]{3,2,1,0:T(8,128)(2,1)S(1)}, bf16[2,4,16,768]{3,2,1,0:T(8,128)(2,1)S(1)}, u32[]{:S(2)}, u32[]{:S(2)}) collective-permute-start(bf16[2,4,16,768]{3,2,1,0:T(8,128)(2,1)S(1)} %add_convert_fusion.9), channel_id=1, source_target_pairs={{0,4},{4,8},{8,12},{12,16},{16,20},{20,24},{24,28},{28,0},{1,5},{5... | collective-permute-start | bytes 589832 | tf_op jit(solution)/shard_map/ppermute | solution.py:127
  108.2 9.0 %collective-permute-done.16 = bf16[2,4,16,768]{3,2,1,0:T(8,128)(2,1)S(1)} collective-permute-done((bf16[2,4,16,768]{3,2,1,0:T(8,128)(2,1)S(1)}, bf16[2,4,16,768]{3,2,1,0:T(8,128)(2,1)S(1)}, u32[]{:S(2)}, u32[]{:S(2)}) %collective-permute-start.16) | collective-permute-done | bytes 196640 | tf_op jit(solution)/shard_map/ppermute | solution.py:127
  117.2 0.1 add_convert_fusion.8
  117.4 0.1 collective-permute-start.17
  117.5 3.2 %collective-permute-start.20 = (bf16[2,4,16,768]{3,2,1,0:T(8,128)(2,1)S(1)}, bf16[2,4,16,768]{3,2,1,0:T(8,128)(2,1)S(1)}, u32[]{:S(2)}, u32[]{:S(2)}) collective-permute-start(bf16[2,4,16,768]{3,2,1,0:T(8,128)(2,1)S(1)} %get-tuple-element.34), channel_id=1, source_target_pairs={{0,28},{4,0},{8,4},{12,8},{16,12},{20,16},{24,20},{28,24},{1,29},{... | collective-permute-start | bytes 589832 | tf_op jit(solution)/shard_map/ppermute | solution.py:127
  120.7 8.3 %collective-permute-done.17 = bf16[2,4,16,768]{3,2,1,0:T(8,128)(2,1)S(1)} collective-permute-done((bf16[2,4,16,768]{3,2,1,0:T(8,128)(2,1)S(1)}, bf16[2,4,16,768]{3,2,1,0:T(8,128)(2,1)S(1)}, u32[]{:S(2)}, u32[]{:S(2)}) %collective-permute-start.17) | collective-permute-done | bytes 196640 | tf_op jit(solution)/shard_map/ppermute | solution.py:127
  129.0 0.1 add_convert_fusion.7
  129.1 0.1 collective-permute-start.18
  129.2 3.2 %collective-permute-start.21 = (bf16[2,4,16,768]{3,2,1,0:T(8,128)(2,1)S(1)}, bf16[2,4,16,768]{3,2,1,0:T(8,128)(2,1)S(1)}, u32[]{:S(2)}, u32[]{:S(2)}) collective-permute-start(bf16[2,4,16,768]{3,2,1,0:T(8,128)(2,1)S(1)} %get-tuple-element.32), channel_id=1, source_target_pairs={{0,28},{4,0},{8,4},{12,8},{16,12},{20,16},{24,20},{28,24},{1,29},{... | collective-permute-start | bytes 589832 | tf_op jit(solution)/shard_map/ppermute | solution.py:127
  132.4 6.3 %collective-permute-done.18 = bf16[2,4,16,768]{3,2,1,0:T(8,128)(2,1)S(1)} collective-permute-done((bf16[2,4,16,768]{3,2,1,0:T(8,128)(2,1)S(1)}, bf16[2,4,16,768]{3,2,1,0:T(8,128)(2,1)S(1)}, u32[]{:S(2)}, u32[]{:S(2)}) %collective-permute-start.18) | collective-permute-done | bytes 196640 | tf_op jit(solution)/shard_map/ppermute | solution.py:127
  138.8 0.5 collective-permute-done.21
  139.3 0.1 add_convert_fusion.6
  139.4 3.8 %collective-permute-start.22 = (bf16[2,4,16,768]{3,2,1,0:T(8,128)(2,1)S(1)}, bf16[2,4,16,768]{3,2,1,0:T(8,128)(2,1)}, u32[]{:S(2)}, u32[]{:S(2)}) collective-permute-start(bf16[2,4,16,768]{3,2,1,0:T(8,128)(2,1)S(1)} %get-tuple-element.30), channel_id=1, source_target_pairs={{0,28},{4,0},{8,4},{12,8},{16,12},{20,16},{24,20},{28,24},{1,29},{... | collective-permute-start | bytes 589832 | tf_op jit(solution)/shard_map/ppermute | solution.py:127
  143.2 5.1 %collective-permute-done.22 = bf16[2,4,16,768]{3,2,1,0:T(8,128)(2,1)} collective-permute-done((bf16[2,4,16,768]{3,2,1,0:T(8,128)(2,1)S(1)}, bf16[2,4,16,768]{3,2,1,0:T(8,128)(2,1)}, u32[]{:S(2)}, u32[]{:S(2)}) %collective-permute-start.22) | collective-permute-done | bytes 196640 | tf_op jit(solution)/shard_map/ppermute | solution.py:127
  148.3 2.4 %collective-permute-done.19 = bf16[2,4,16,768]{3,2,1,0:T(8,128)(2,1)} collective-permute-done((bf16[2,4,16,768]{3,2,1,0:T(8,128)(2,1)S(1)}, bf16[2,4,16,768]{3,2,1,0:T(8,128)(2,1)}, u32[]{:S(2)}, u32[]{:S(2)}) %collective-permute-start.19) | collective-permute-done | bytes 196640 | tf_op jit(solution)/shard_map/ppermute | solution.py:127
  150.7 1.1 add_convert_fusion.2
  151.9 0.0 reduce-scatter.2.cloned.1.call-done
  151.9 0.9 fusion.9
  152.8 0.1 maximum_bitcast_fusion
  152.9 0.1 reverse_select_fusion
  153.0 0.2 fusion.7
  153.2 15.3 %all_to_all.5 = bf16[16,16,768]{2,1,0:T(8,128)(2,1)S(1)} all-to-all(bf16[16,16,768]{2,1,0:T(8,128)(2,1)S(1)} %bitcast.35), channel_id=1, replica_groups=mesh['y_lo'=2,'x'=4,'z'=8,'y_hi'=2,'core'=2] {'y_hi','y_lo','x'}, dimensions={0} | all-to-all | bytes 786432 | tf_op jit(solution)/shard_map/all_to_all | solution.py:197
  168.6 0.7 copy.11
  (42 shorter events, 0.3 us)
Async XLA Ops:
  6.5 145.4 %reduce-scatter.2.cloned.1.call-start = ((), (), s32[]{:S(2)}) async-start(), calls=%async_computation.2 | async-start | bytes 1769472 | tf_op jit(solution)/shard_map/reduce_scatter | solution.py:170
  7.2 12.6 %copy-start.5 = (f32[512]{0:T(512)S(1)}, f32[512]{0:T(512)}, u32[]{:S(2)}) copy-start(f32[512]{0:T(512)} %param.7) | copy-start | bytes 6148
  7.2 12.8 %copy-start.3 = (bf16[512,2,256]{2,1,0:T(2,128)(2,1)S(1)}, bf16[512,2,256]{2,1,0:T(2,128)(2,1)}, u32[]{:S(2)}) copy-start(bf16[512,2,256]{2,1,0:T(2,128)(2,1)} %param.6) | copy-start | bytes 1572868
  7.2 12.8 %copy-start.4 = (bf16[512,2,256]{2,1,0:T(2,128)(2,1)S(1)}, bf16[512,2,256]{2,1,0:T(2,128)(2,1)}, u32[]{:S(2)}) copy-start(bf16[512,2,256]{2,1,0:T(2,128)(2,1)} %param.5) | copy-start | bytes 1572868
  11.0 11.2 %collective-permute-start.3 = (bf16[256,768]{1,0:T(8,128)(2,1)}, bf16[256,768]{1,0:T(8,128)(2,1)S(1)}, u32[]{:S(2)}, u32[]{:S(2)}) collective-permute-start(bf16[256,768]{1,0:T(8,128)(2,1)} %get-tuple-element.18), channel_id=1, source_target_pairs={{0,128},{32,160},{64,192},{96,224},{128,0},{160,32},{192,64},{224,... | collective-permute-start | bytes 1179656 | tf_op jit(solution)/shard_map/ppermute | solution.py:161
  12.6 13.9 %collective-permute-start.4 = (bf16[256,768]{1,0:T(8,128)(2,1)}, bf16[256,768]{1,0:T(8,128)(2,1)S(1)}, u32[]{:S(2)}, u32[]{:S(2)}) collective-permute-start(bf16[256,768]{1,0:T(8,128)(2,1)} %get-tuple-element.19), channel_id=1, source_target_pairs={{0,64},{32,96},{64,0},{96,32},{128,192},{160,224},{192,128},{224,1... | collective-permute-start | bytes 1179656 | tf_op jit(solution)/shard_map/ppermute | solution.py:161
  14.7 20.0 %collective-permute-start.5 = (bf16[256,768]{1,0:T(8,128)(2,1)}, bf16[256,768]{1,0:T(8,128)(2,1)S(1)}, u32[]{:S(2)}, u32[]{:S(2)}) collective-permute-start(bf16[256,768]{1,0:T(8,128)(2,1)} %get-tuple-element.20), channel_id=1, source_target_pairs={{0,192},{32,224},{64,128},{96,160},{128,64},{160,96},{192,0},{224,... | collective-permute-start | bytes 1179656 | tf_op jit(solution)/shard_map/ppermute | solution.py:161
  16.0 27.3 %collective-permute-start.6 = (bf16[256,768]{1,0:T(8,128)(2,1)}, bf16[256,768]{1,0:T(8,128)(2,1)S(1)}, u32[]{:S(2)}, u32[]{:S(2)}) collective-permute-start(bf16[256,768]{1,0:T(8,128)(2,1)} %get-tuple-element.21), channel_id=1, source_target_pairs={{0,32},{32,64},{64,96},{96,0},{128,160},{160,192},{192,224},{224,1... | collective-permute-start | bytes 1179656 | tf_op jit(solution)/shard_map/ppermute | solution.py:161
  17.5 34.3 %collective-permute-start.7 = (bf16[256,768]{1,0:T(8,128)(2,1)}, bf16[256,768]{1,0:T(8,128)(2,1)}, u32[]{:S(2)}, u32[]{:S(2)}) collective-permute-start(bf16[256,768]{1,0:T(8,128)(2,1)} %get-tuple-element.22), channel_id=1, source_target_pairs={{0,160},{32,192},{64,224},{96,128},{128,32},{160,64},{192,96},{224... | collective-permute-start | bytes 1179656 | tf_op jit(solution)/shard_map/ppermute | solution.py:161
  19.8 3.1 %copy-start.6 = (s32[512,2]{0,1:T(2,128)S(1)}, s32[512,2]{0,1:T(2,128)}, u32[]{:S(2)}) copy-start(s32[512,2]{0,1:T(2,128)} %param.8) | copy-start | bytes 12292
  19.9 2.2 %copy-start.13 = (bf16[256,768]{1,0:T(8,128)(2,1)S(1)}, bf16[256,768]{1,0:T(8,128)(2,1)}, u32[]{:S(2)}) copy-start(bf16[256,768]{1,0:T(8,128)(2,1)} %get-tuple-element.23) | copy-start | bytes 1179652
  22.1 53.6 %copy-start.9 = (bf16[256,768]{1,0:T(8,128)(2,1)}, bf16[256,768]{1,0:T(8,128)(2,1)S(1)}, u32[]{:S(2)}) copy-start(bf16[256,768]{1,0:T(8,128)(2,1)S(1)} %collective-permute-done.3.refs_6_) | copy-start | bytes 1179652
  22.1 31.0 %collective-permute-start.8 = (bf16[256,768]{1,0:T(8,128)(2,1)S(1)}, bf16[256,768]{1,0:T(8,128)(2,1)}, u32[]{:S(2)}, u32[]{:S(2)}) collective-permute-start(bf16[256,768]{1,0:T(8,128)(2,1)S(1)} %copy-done.13), channel_id=1, source_target_pairs={{0,96},{32,0},{64,32},{96,64},{128,224},{160,128},{192,160},{224,1... | collective-permute-start | bytes 1179656 | tf_op jit(solution)/shard_map/ppermute | solution.py:161
  22.9 52.8 %copy-start.2 = (bf16[528,512]{1,0:T(8,128)(2,1)}, bf16[528,512]{1,0:T(8,128)(2,1)S(1)}, u32[]{:S(2)}) copy-start(bf16[528,512]{1,0:T(8,128)(2,1)S(1)} %fusion.6.refs_1_) | copy-start | bytes 1622020
  26.5 49.3 %copy-start.10 = (bf16[256,768]{1,0:T(8,128)(2,1)}, bf16[256,768]{1,0:T(8,128)(2,1)S(1)}, u32[]{:S(2)}) copy-start(bf16[256,768]{1,0:T(8,128)(2,1)S(1)} %collective-permute-done.4.refs_7_) | copy-start | bytes 1179652
  26.5 29.1 %collective-permute-start = (bf16[528,512]{1,0:T(8,128)(2,1)S(1)}, bf16[528,512]{1,0:T(8,128)(2,1)}, u32[]{:S(2)}, u32[]{:S(2)}) collective-permute-start(bf16[528,512]{1,0:T(8,128)(2,1)S(1)} %fusion.6.refs_1_), channel_id=1, source_target_pairs={{0,128},{128,0},{1,129},{129,1},{2,130},{130,2},{3,131},{131,3},{4... | collective-permute-start | bytes 1622024 | tf_op jit(solution)/shard_map/ppermute | solution.py:127
  34.8 41.0 %copy-start.11 = (bf16[256,768]{1,0:T(8,128)(2,1)}, bf16[256,768]{1,0:T(8,128)(2,1)S(1)}, u32[]{:S(2)}) copy-start(bf16[256,768]{1,0:T(8,128)(2,1)S(1)} %collective-permute-done.5.refs_8_) | copy-start | bytes 1179652
  34.8 39.3 %collective-permute-start.13 = (bf16[528,512]{1,0:T(8,128)(2,1)S(1)}, bf16[528,512]{1,0:T(8,128)(2,1)}, u32[]{:S(2)}, u32[]{:S(2)}) collective-permute-start(bf16[528,512]{1,0:T(8,128)(2,1)S(1)} %fusion.6.refs_1_), channel_id=1, source_target_pairs={{0,64},{32,96},{64,0},{96,32},{1,65},{33,97},{65,1},{97,33},{2,66}... | collective-permute-start | bytes 1622024 | tf_op jit(solution)/shard_map/ppermute | solution.py:127
  43.3 32.4 %copy-start.12 = (bf16[256,768]{1,0:T(8,128)(2,1)}, bf16[256,768]{1,0:T(8,128)(2,1)S(1)}, u32[]{:S(2)}) copy-start(bf16[256,768]{1,0:T(8,128)(2,1)S(1)} %collective-permute-done.6.refs_9_) | copy-start | bytes 1179652
  43.3 32.3 %collective-permute-start.1 = (bf16[528,512]{1,0:T(8,128)(2,1)S(1)}, bf16[528,512]{1,0:T(8,128)(2,1)S(1)}, u32[]{:S(2)}, u32[]{:S(2)}) collective-permute-start(bf16[528,512]{1,0:T(8,128)(2,1)S(1)} %fusion.6.refs_1_), channel_id=1, source_target_pairs={{0,96},{32,0},{64,32},{96,64},{1,97},{33,1},{65,33},{97,65},{2,98}... | collective-permute-start | bytes 1622024 | tf_op jit(solution)/shard_map/ppermute | solution.py:127
  51.8 23.9 %collective-permute-start.2 = (bf16[528,512]{1,0:T(8,128)(2,1)S(1)}, bf16[528,512]{1,0:T(8,128)(2,1)S(1)}, u32[]{:S(2)}, u32[]{:S(2)}) collective-permute-start(bf16[528,512]{1,0:T(8,128)(2,1)S(1)} %fusion.6.refs_1_), channel_id=1, source_target_pairs={{0,32},{32,64},{64,96},{96,0},{1,33},{33,65},{65,97},{97,1},{2,34}... | collective-permute-start | bytes 1622024 | tf_op jit(solution)/shard_map/ppermute | solution.py:127
  53.1 20.4 %collective-permute-start.9 = (bf16[256,768]{1,0:T(8,128)(2,1)}, bf16[256,768]{1,0:T(8,128)(2,1)}, u32[]{:S(2)}, u32[]{:S(2)}) collective-permute-start(bf16[256,768]{1,0:T(8,128)(2,1)} %get-tuple-element.24), channel_id=1, source_target_pairs={{0,224},{32,128},{64,160},{96,192},{128,96},{160,0},{192,32},{224,... | collective-permute-start | bytes 1179656 | tf_op jit(solution)/shard_map/ppermute | solution.py:161
  55.5 33.4 %collective-permute-start.11 = (bf16[528,512]{1,0:T(8,128)(2,1)}, bf16[528,512]{1,0:T(8,128)(2,1)}, u32[]{:S(2)}, u32[]{:S(2)}) collective-permute-start(bf16[528,512]{1,0:T(8,128)(2,1)} %collective-permute-done.refs_2_), channel_id=1, source_target_pairs={{0,32},{32,64},{64,96},{96,0},{1,33},{33,65},{65,97},{97,1},{2,34}... | collective-permute-start | bytes 1622024 | tf_op jit(solution)/shard_map/ppermute | solution.py:127
  73.4 15.5 %collective-permute-start.12 = (bf16[528,512]{1,0:T(8,128)(2,1)}, bf16[528,512]{1,0:T(8,128)(2,1)}, u32[]{:S(2)}, u32[]{:S(2)}) collective-permute-start(bf16[528,512]{1,0:T(8,128)(2,1)} %collective-permute-done.refs_2_), channel_id=1, source_target_pairs={{0,96},{32,0},{64,32},{96,64},{1,97},{33,1},{65,33},{97,65},{2,98}... | collective-permute-start | bytes 1622024 | tf_op jit(solution)/shard_map/ppermute | solution.py:127
  74.1 14.9 %collective-permute-start.14 = (bf16[528,512]{1,0:T(8,128)(2,1)}, bf16[528,512]{1,0:T(8,128)(2,1)}, u32[]{:S(2)}, u32[]{:S(2)}) collective-permute-start(bf16[528,512]{1,0:T(8,128)(2,1)} %collective-permute-done.13.refs_4_), channel_id=1, source_target_pairs={{0,128},{128,0},{1,129},{129,1},{2,130},{130,2},{3,131},{131,3},{4... | collective-permute-start | bytes 1622024 | tf_op jit(solution)/shard_map/ppermute | solution.py:127
  75.7 0.8 copy-start.7
  75.7 1.0 copy-start.8
  88.6 13.0 %collective-permute-start.10 = (bf16[16,4,16,768]{3,2,1,0:T(8,128)(2,1)}, bf16[16,4,16,768]{3,2,1,0:T(8,128)(2,1)}, u32[]{:S(2)}, u32[]{:S(2)}) collective-permute-start(bf16[16,4,16,768]{3,2,1,0:T(8,128)(2,1)} %get-tuple-element.26), channel_id=1, source_target_pairs={{0,1},{1,0},{2,3},{3,2},{4,5},{5,4},{6,7},{7,6},{8,9},{9,8},{10,11... | collective-permute-start | bytes 4718600 | tf_op jit(solution)/shard_map/ppermute | solution.py:167
  89.0 12.7 %copy-start = (bf16[16,4,16,768]{3,2,1,0:T(8,128)(2,1)S(1)}, bf16[16,4,16,768]{3,2,1,0:T(8,128)(2,1)}, u32[]{:S(2)}) copy-start(bf16[16,4,16,768]{3,2,1,0:T(8,128)(2,1)} %get-tuple-element.25) | copy-start | bytes 4718596
  101.1 3.8 %collective-permute-start.15 = (bf16[16,4,16,768]{3,2,1,0:T(8,128)(2,1)}, bf16[16,4,16,768]{3,2,1,0:T(8,128)(2,1)S(1)}, u32[]{:S(2)}, u32[]{:S(2)}) collective-permute-start(bf16[16,4,16,768]{3,2,1,0:T(8,128)(2,1)} %get-tuple-element.28), channel_id=1, source_target_pairs={{0,1},{1,0},{2,3},{3,2},{4,5},{5,4},{6,7},{7,6},{8,9},{9,8},{10,11... | collective-permute-start | bytes 4718600 | tf_op jit(solution)/shard_map/ppermute | solution.py:167
  104.8 1.4 copy-start.1
  106.2 11.0 %collective-permute-start.16 = (bf16[2,4,16,768]{3,2,1,0:T(8,128)(2,1)S(1)}, bf16[2,4,16,768]{3,2,1,0:T(8,128)(2,1)S(1)}, u32[]{:S(2)}, u32[]{:S(2)}) collective-permute-start(bf16[2,4,16,768]{3,2,1,0:T(8,128)(2,1)S(1)} %add_convert_fusion.9), channel_id=1, source_target_pairs={{0,4},{4,8},{8,12},{12,16},{16,20},{20,24},{24,28},{28,0},{1,5},{5... | collective-permute-start | bytes 589832 | tf_op jit(solution)/shard_map/ppermute | solution.py:127
  117.4 11.6 %collective-permute-start.17 = (bf16[2,4,16,768]{3,2,1,0:T(8,128)(2,1)S(1)}, bf16[2,4,16,768]{3,2,1,0:T(8,128)(2,1)S(1)}, u32[]{:S(2)}, u32[]{:S(2)}) collective-permute-start(bf16[2,4,16,768]{3,2,1,0:T(8,128)(2,1)S(1)} %get-tuple-element.33), channel_id=1, source_target_pairs={{0,4},{4,8},{8,12},{12,16},{16,20},{20,24},{24,28},{28,0},{1,5},{5... | collective-permute-start | bytes 589832 | tf_op jit(solution)/shard_map/ppermute | solution.py:127
  117.5 11.5 %collective-permute-start.20 = (bf16[2,4,16,768]{3,2,1,0:T(8,128)(2,1)S(1)}, bf16[2,4,16,768]{3,2,1,0:T(8,128)(2,1)S(1)}, u32[]{:S(2)}, u32[]{:S(2)}) collective-permute-start(bf16[2,4,16,768]{3,2,1,0:T(8,128)(2,1)S(1)} %get-tuple-element.34), channel_id=1, source_target_pairs={{0,28},{4,0},{8,4},{12,8},{16,12},{20,16},{24,20},{28,24},{1,29},{... | collective-permute-start | bytes 589832 | tf_op jit(solution)/shard_map/ppermute | solution.py:127
  129.1 9.6 %collective-permute-start.18 = (bf16[2,4,16,768]{3,2,1,0:T(8,128)(2,1)S(1)}, bf16[2,4,16,768]{3,2,1,0:T(8,128)(2,1)S(1)}, u32[]{:S(2)}, u32[]{:S(2)}) collective-permute-start(bf16[2,4,16,768]{3,2,1,0:T(8,128)(2,1)S(1)} %get-tuple-element.31), channel_id=1, source_target_pairs={{0,4},{4,8},{8,12},{12,16},{16,20},{20,24},{24,28},{28,0},{1,5},{5... | collective-permute-start | bytes 589832 | tf_op jit(solution)/shard_map/ppermute | solution.py:127
  129.2 10.1 %collective-permute-start.21 = (bf16[2,4,16,768]{3,2,1,0:T(8,128)(2,1)S(1)}, bf16[2,4,16,768]{3,2,1,0:T(8,128)(2,1)S(1)}, u32[]{:S(2)}, u32[]{:S(2)}) collective-permute-start(bf16[2,4,16,768]{3,2,1,0:T(8,128)(2,1)S(1)} %get-tuple-element.32), channel_id=1, source_target_pairs={{0,28},{4,0},{8,4},{12,8},{16,12},{20,16},{24,20},{28,24},{1,29},{... | collective-permute-start | bytes 589832 | tf_op jit(solution)/shard_map/ppermute | solution.py:127
  139.4 8.9 %collective-permute-start.22 = (bf16[2,4,16,768]{3,2,1,0:T(8,128)(2,1)S(1)}, bf16[2,4,16,768]{3,2,1,0:T(8,128)(2,1)}, u32[]{:S(2)}, u32[]{:S(2)}) collective-permute-start(bf16[2,4,16,768]{3,2,1,0:T(8,128)(2,1)S(1)} %get-tuple-element.30), channel_id=1, source_target_pairs={{0,28},{4,0},{8,4},{12,8},{16,12},{20,16},{24,20},{28,24},{1,29},{... | collective-permute-start | bytes 589832 | tf_op jit(solution)/shard_map/ppermute | solution.py:127
  143.2 7.5 %collective-permute-start.19 = (bf16[2,4,16,768]{3,2,1,0:T(8,128)(2,1)S(1)}, bf16[2,4,16,768]{3,2,1,0:T(8,128)(2,1)}, u32[]{:S(2)}, u32[]{:S(2)}) collective-permute-start(bf16[2,4,16,768]{3,2,1,0:T(8,128)(2,1)S(1)} %get-tuple-element.29), channel_id=1, source_target_pairs={{0,4},{4,8},{8,12},{12,16},{16,20},{20,24},{24,28},{28,0},{1,5},{5... | collective-permute-start | bytes 589832 | tf_op jit(solution)/shard_map/ppermute | solution.py:127
Sparse Core Ops, SparseCore 0:
  104.9 45.6 reduce-scatter.1

commit v3 on v2

--- a/solution.py
+++ b/solution.py
@@ -108,7 +108,7 @@
     return pl.pallas_call(
         cut_kernel,
         in_specs=[SMEM, VMEM],
-        out_specs=[HBM] * parts,
+        out_specs=[VMEM] * parts,
         out_shape=[shape] * parts,
         scratch_shapes=[pltpu.SemaphoreType.DMA((parts,))],
         compiler_params=pltpu.CompilerParams(vmem_limit_bytes=LIMIT),

time: 176 us -> 177 us (level)
  transfers between devices with their start and end apart: 24 -> 24, of which waited for: 13 -> 12; matrix products, arithmetic and copies ran while one was open for 4% -> 4% of each run, Pallas kernels for 14% -> 14%
where the time goes in v3:
time: 177 us
  waiting for transfers between devices  74.8 us (42%)
  starting transfers between devices  32.2 us (18%)
  Pallas kernels  28.2 us (16%)
  blocking collectives  15.5 us (9%)
  between operations  13.7 us (8%)
  other arithmetic  6.73 us (4%)
  local copies, waits for them, and re-layouts  5.38 us (3%)
    ppermute x7, waiting for transfers between devices, on_device(): weights[i] = lax.ppermute(weights[i], ('y_lo', 'x'), pairs)  43.4 us
    ppermute x14, waiting for transfers between devices, shift(): lax.ppermute(value, axis, [(i, (i + by) % size) for i in range(size)])  31.3 us
    pallas_call x2, Pallas kernels, mix(): pl.pallas_call(lambda *refs: mix_kernel(count, experts, turned, *refs), i...  24.1 us
    ppermute x14, starting transfers between devices, shift(): lax.ppermute(value, axis, [(i, (i + by) % size) for i in range(size)])  20 us
    all_to_all x1, blocking collectives, on_device(): pieces = lax.all_to_all(pieces, ('y_hi', 'y_lo', 'x'), 0, 0, tiled=True)  15.5 us
    ppermute x7, starting transfers between devices, on_device(): weights[i] = lax.ppermute(weights[i], ('y_lo', 'x'), pairs)  11.3 us
    convert_element_type x6, other arithmetic, wide_sum(): return sum((t.astype(jnp.float32) for t in terms)).astype(jnp.bfloat16)  4.67 us
    pallas_call x1, Pallas kernels, cut(): pl.pallas_call(cut_kernel, in_specs=[SMEM, VMEM], out_specs=[VMEM] * part...  4.1 us
  transfers between devices with their start and end apart: 24, of which 12 were waited for; matrix products, arithmetic and copies ran while one was open for 4% of the time, Pallas kernels for 14%

profile of v3, /device:TPU:2, one launch (start us, length us, event | category | flops | bytes accessed | tf_op | source)
XLA Modules:
  0.0 176.6 jit_solution(5580409350123312871)
XLA Ops:
  6.5 0.6 stack.101.order_ref
  7.2 4.1 %shard_map.55 = (bf16[256,768]{1,0:T(8,128)(2,1)}, bf16[256,768]{1,0:T(8,128)(2,1)}, bf16[256,768]{1,0:T(8,128)(2,1)}, bf16[256,768]{1,0:T(8,128)(2,1)}, bf16[25...) custom-call(s32[8]{0:T(128)} %stack.101.order_ref, ...), custom_call_target="tpu_custom_call" | custom-call | bytes 6291456 | tf_op jit(solution)/shard_map/pallas_call | solution.py:108
  11.3 1.7 collective-permute-start.3
  12.9 2.1 %collective-permute-start.4 = (bf16[256,768]{1,0:T(8,128)(2,1)}, bf16[256,768]{1,0:T(8,128)(2,1)S(1)}, u32[]{:S(2)}, u32[]{:S(2)}) collective-permute-start(bf16[256,768]{1,0:T(8,128)(2,1)} %get-tuple-element.19), channel_id=1, source_target_pairs={{0,64},{32,96},{64,0},{96,32},{128,192},{160,224},{192,128},{224,1... | collective-permute-start | bytes 1179656 | tf_op jit(solution)/shard_map/ppermute | solution.py:161
  15.1 1.3 collective-permute-start.5
  16.4 1.5 collective-permute-start.6
  17.9 2.2 %collective-permute-start.7 = (bf16[256,768]{1,0:T(8,128)(2,1)}, bf16[256,768]{1,0:T(8,128)(2,1)}, u32[]{:S(2)}, u32[]{:S(2)}) collective-permute-start(bf16[256,768]{1,0:T(8,128)(2,1)} %get-tuple-element.22), channel_id=1, source_target_pairs={{0,160},{32,192},{64,224},{96,128},{128,32},{160,64},{192,96},{224... | collective-permute-start | bytes 1179656 | tf_op jit(solution)/shard_map/ppermute | solution.py:161
  20.1 0.0 copy-start.6
  20.1 0.1 copy.8
  20.3 1.6 fusion.5
  21.9 0.1 copy.12
  22.0 0.4 collective-permute-done.3.refs_6_
  22.4 0.8 collective-permute-start.8
  23.3 3.5 %collective-permute-done.4.refs_7_ = bf16[256,768]{1,0:T(8,128)(2,1)S(1)} collective-permute-done((bf16[256,768]{1,0:T(8,128)(2,1)}, bf16[256,768]{1,0:T(8,128)(2,1)S(1)}, u32[]{:S(2)}, u32[]{:S(2)}) %collective-permute-start.4) | collective-permute-done | bytes 393248 | tf_op jit(solution)/shard_map/ppermute | solution.py:161
  26.8 0.4 collective-permute-start
  27.3 7.8 %collective-permute-done.5.refs_8_ = bf16[256,768]{1,0:T(8,128)(2,1)S(1)} collective-permute-done((bf16[256,768]{1,0:T(8,128)(2,1)}, bf16[256,768]{1,0:T(8,128)(2,1)S(1)}, u32[]{:S(2)}, u32[]{:S(2)}) %collective-permute-start.5) | collective-permute-done | bytes 393248 | tf_op jit(solution)/shard_map/ppermute | solution.py:161
  35.1 2.1 %collective-permute-start.13 = (bf16[528,512]{1,0:T(8,128)(2,1)S(1)}, bf16[528,512]{1,0:T(8,128)(2,1)}, u32[]{:S(2)}, u32[]{:S(2)}) collective-permute-start(bf16[528,512]{1,0:T(8,128)(2,1)S(1)} %fusion.6.refs_1_), channel_id=1, source_target_pairs={{0,64},{32,96},{64,0},{96,32},{1,65},{33,97},{65,1},{97,33},{2,66}... | collective-permute-start | bytes 1622024 | tf_op jit(solution)/shard_map/ppermute | solution.py:127
  37.2 6.5 %collective-permute-done.6.refs_9_ = bf16[256,768]{1,0:T(8,128)(2,1)S(1)} collective-permute-done((bf16[256,768]{1,0:T(8,128)(2,1)}, bf16[256,768]{1,0:T(8,128)(2,1)S(1)}, u32[]{:S(2)}, u32[]{:S(2)}) %collective-permute-start.6) | collective-permute-done | bytes 393248 | tf_op jit(solution)/shard_map/ppermute | solution.py:161
  43.7 0.0 collective-permute-start.1
  43.7 8.4 %collective-permute-done.7.refs_10_ = bf16[256,768]{1,0:T(8,128)(2,1)} collective-permute-done((bf16[256,768]{1,0:T(8,128)(2,1)}, bf16[256,768]{1,0:T(8,128)(2,1)}, u32[]{:S(2)}, u32[]{:S(2)}) %collective-permute-start.7) | collective-permute-done | bytes 393248 | tf_op jit(solution)/shard_map/ppermute | solution.py:161
  52.1 1.3 collective-permute-start.2
  53.4 1.8 %collective-permute-start.9 = (bf16[256,768]{1,0:T(8,128)(2,1)}, bf16[256,768]{1,0:T(8,128)(2,1)}, u32[]{:S(2)}, u32[]{:S(2)}) collective-permute-start(bf16[256,768]{1,0:T(8,128)(2,1)} %get-tuple-element.24), channel_id=1, source_target_pairs={{0,224},{32,128},{64,160},{96,192},{128,96},{160,0},{192,32},{224,... | collective-permute-start | bytes 1179656 | tf_op jit(solution)/shard_map/ppermute | solution.py:161
  55.2 0.7 stack.91.refs_0_
  55.9 0.0 collective-permute-done.refs_2_
  55.9 1.3 collective-permute-start.11
  57.1 16.6 %collective-permute-done.9.refs_12_ = bf16[256,768]{1,0:T(8,128)(2,1)} collective-permute-done((bf16[256,768]{1,0:T(8,128)(2,1)}, bf16[256,768]{1,0:T(8,128)(2,1)}, u32[]{:S(2)}, u32[]{:S(2)}) %collective-permute-start.9) | collective-permute-done | bytes 393248 | tf_op jit(solution)/shard_map/ppermute | solution.py:161
  73.8 0.6 collective-permute-start.12
  74.4 0.0 collective-permute-done.13.refs_4_
  74.4 1.6 collective-permute-start.14
  76.0 0.0 collective-permute-done.1.refs_3_
  76.1 0.7 copy-done.7
  76.8 0.2 copy-done.8
  77.0 12.0 %shard_map.56 = (bf16[16,4,16,768]{3,2,1,0:T(8,128)(2,1)}, bf16[16,4,16,768]{3,2,1,0:T(8,128)(2,1)}) custom-call(s32[10]{0:T(128)} %stack.91.refs_0_, bf16[528,512]{1,0:T(8,128)(2,1)} %copy-done.2, bf16[528,512]{1,0:T(8,128)(2,1)} %collective-permute-done.refs_2_, bf16[528,512]{1,0:T(8,128)(2,1)} %copy-done.7, bf16[528,512]{1,0:T(8,128)(2,1)} %copy-done.8, ...), custom_call_target="tpu_custom_call" | custom-call | flops 999999995904 | bytes 1000 | tf_op jit(solution)/shard_map/pallas_call | solution.py:70
  89.0 0.3 collective-permute-start.10
  89.3 12.1 %shard_map.57 = (bf16[16,4,16,768]{3,2,1,0:T(8,128)(2,1)}, bf16[16,4,16,768]{3,2,1,0:T(8,128)(2,1)}) custom-call(s32[10]{0:T(128)} %stack.91.refs_0_, bf16[528,512]{1,0:T(8,128)(2,1)} %collective-permute-done.11.refs_1_, bf16[528,512]{1,0:T(8,128)(2,1)} %collective-permute-done.12.refs_2_, bf16[528,512]{1,0:T(8,128)(2,1)} %collective-permute-done.14.refs_3_, ...), custom_call_target="tpu_custom_call" | custom-call | flops 999999995904 | bytes 1000 | tf_op jit(solution)/shard_map/pallas_call | solution.py:70
  101.4 0.6 collective-permute-start.15
  102.0 3.1 %add_convert_fusion = bf16[16,4,16,768]{3,2,1,0:T(8,128)(2,1)} fusion(bf16[16,4,16,768]{3,2,1,0:T(8,128)(2,1)} %collective-permute-done.10, bf16[16,4,16,768]{3,2,1,0:T(8,128)(2,1)S(1)} %copy-done), kind=kLoop, calls=%fused_computation | loop fusion | flops 3145728 | bytes 4718592 | tf_op jit(solution)/shard_map/convert_element_type | solution.py:122
  105.1 0.0 reduce-scatter.2.cloned.1.call-update
  105.1 0.1 collective-permute-done.15
  105.3 1.2 copy-done.1
  106.6 2.0 %collective-permute-start.16 = (bf16[2,4,16,768]{3,2,1,0:T(8,128)(2,1)S(1)}, bf16[2,4,16,768]{3,2,1,0:T(8,128)(2,1)S(1)}, u32[]{:S(2)}, u32[]{:S(2)}) collective-permute-start(bf16[2,4,16,768]{3,2,1,0:T(8,128)(2,1)S(1)} %add_convert_fusion.9), channel_id=1, source_target_pairs={{0,4},{4,8},{8,12},{12,16},{16,20},{20,24},{24,28},{28,0},{1,5},{5... | collective-permute-start | bytes 589832 | tf_op jit(solution)/shard_map/ppermute | solution.py:127
  108.5 9.0 %collective-permute-done.16 = bf16[2,4,16,768]{3,2,1,0:T(8,128)(2,1)S(1)} collective-permute-done((bf16[2,4,16,768]{3,2,1,0:T(8,128)(2,1)S(1)}, bf16[2,4,16,768]{3,2,1,0:T(8,128)(2,1)S(1)}, u32[]{:S(2)}, u32[]{:S(2)}) %collective-permute-start.16) | collective-permute-done | bytes 196640 | tf_op jit(solution)/shard_map/ppermute | solution.py:127
  117.6 0.1 add_convert_fusion.8
  117.7 0.1 collective-permute-start.17
  117.8 3.2 %collective-permute-start.20 = (bf16[2,4,16,768]{3,2,1,0:T(8,128)(2,1)S(1)}, bf16[2,4,16,768]{3,2,1,0:T(8,128)(2,1)S(1)}, u32[]{:S(2)}, u32[]{:S(2)}) collective-permute-start(bf16[2,4,16,768]{3,2,1,0:T(8,128)(2,1)S(1)} %get-tuple-element.34), channel_id=1, source_target_pairs={{0,28},{4,0},{8,4},{12,8},{16,12},{20,16},{24,20},{28,24},{1,29},{... | collective-permute-start | bytes 589832 | tf_op jit(solution)/shard_map/ppermute | solution.py:127
  121.0 8.3 %collective-permute-done.17 = bf16[2,4,16,768]{3,2,1,0:T(8,128)(2,1)S(1)} collective-permute-done((bf16[2,4,16,768]{3,2,1,0:T(8,128)(2,1)S(1)}, bf16[2,4,16,768]{3,2,1,0:T(8,128)(2,1)S(1)}, u32[]{:S(2)}, u32[]{:S(2)}) %collective-permute-start.17) | collective-permute-done | bytes 196640 | tf_op jit(solution)/shard_map/ppermute | solution.py:127
  129.3 0.1 add_convert_fusion.7
  129.4 0.1 collective-permute-start.18
  129.5 3.2 %collective-permute-start.21 = (bf16[2,4,16,768]{3,2,1,0:T(8,128)(2,1)S(1)}, bf16[2,4,16,768]{3,2,1,0:T(8,128)(2,1)S(1)}, u32[]{:S(2)}, u32[]{:S(2)}) collective-permute-start(bf16[2,4,16,768]{3,2,1,0:T(8,128)(2,1)S(1)} %get-tuple-element.32), channel_id=1, source_target_pairs={{0,28},{4,0},{8,4},{12,8},{16,12},{20,16},{24,20},{28,24},{1,29},{... | collective-permute-start | bytes 589832 | tf_op jit(solution)/shard_map/ppermute | solution.py:127
  132.8 6.5 %collective-permute-done.18 = bf16[2,4,16,768]{3,2,1,0:T(8,128)(2,1)S(1)} collective-permute-done((bf16[2,4,16,768]{3,2,1,0:T(8,128)(2,1)S(1)}, bf16[2,4,16,768]{3,2,1,0:T(8,128)(2,1)S(1)}, u32[]{:S(2)}, u32[]{:S(2)}) %collective-permute-start.18) | collective-permute-done | bytes 196640 | tf_op jit(solution)/shard_map/ppermute | solution.py:127
  139.3 0.0 collective-permute-done.21
  139.3 0.1 add_convert_fusion.6
  139.5 3.8 %collective-permute-start.22 = (bf16[2,4,16,768]{3,2,1,0:T(8,128)(2,1)S(1)}, bf16[2,4,16,768]{3,2,1,0:T(8,128)(2,1)}, u32[]{:S(2)}, u32[]{:S(2)}) collective-permute-start(bf16[2,4,16,768]{3,2,1,0:T(8,128)(2,1)S(1)} %get-tuple-element.30), channel_id=1, source_target_pairs={{0,28},{4,0},{8,4},{12,8},{16,12},{20,16},{24,20},{28,24},{1,29},{... | collective-permute-start | bytes 589832 | tf_op jit(solution)/shard_map/ppermute | solution.py:127
  143.2 0.3 collective-permute-start.19
  143.6 5.4 %collective-permute-done.22 = bf16[2,4,16,768]{3,2,1,0:T(8,128)(2,1)} collective-permute-done((bf16[2,4,16,768]{3,2,1,0:T(8,128)(2,1)S(1)}, bf16[2,4,16,768]{3,2,1,0:T(8,128)(2,1)}, u32[]{:S(2)}, u32[]{:S(2)}) %collective-permute-start.22) | collective-permute-done | bytes 196640 | tf_op jit(solution)/shard_map/ppermute | solution.py:127
  149.0 2.0 %collective-permute-done.19 = bf16[2,4,16,768]{3,2,1,0:T(8,128)(2,1)} collective-permute-done((bf16[2,4,16,768]{3,2,1,0:T(8,128)(2,1)S(1)}, bf16[2,4,16,768]{3,2,1,0:T(8,128)(2,1)}, u32[]{:S(2)}, u32[]{:S(2)}) %collective-permute-start.19) | collective-permute-done | bytes 196640 | tf_op jit(solution)/shard_map/ppermute | solution.py:127
  151.0 1.1 add_convert_fusion.2
  152.1 0.0 reduce-scatter.2.cloned.1.call-done
  152.2 0.9 fusion.9
  153.0 0.1 maximum_bitcast_fusion
  153.2 0.1 reverse_select_fusion
  153.2 0.2 fusion.7
  153.4 15.5 %all_to_all.5 = bf16[16,16,768]{2,1,0:T(8,128)(2,1)S(1)} all-to-all(bf16[16,16,768]{2,1,0:T(8,128)(2,1)S(1)} %bitcast.35), channel_id=1, replica_groups=mesh['y_lo'=2,'x'=4,'z'=8,'y_hi'=2,'core'=2] {'y_hi','y_lo','x'}, dimensions={0} | all-to-all | bytes 786432 | tf_op jit(solution)/shard_map/all_to_all | solution.py:197
  169.0 0.7 copy.11
  (42 shorter events, 0.3 us)
Async XLA Ops:
  6.5 145.6 %reduce-scatter.2.cloned.1.call-start = ((), (), s32[]{:S(2)}) async-start(), calls=%async_computation.2 | async-start | bytes 1769472 | tf_op jit(solution)/shard_map/reduce_scatter | solution.py:170
  7.2 12.9 %copy-start.5 = (f32[512]{0:T(512)S(1)}, f32[512]{0:T(512)}, u32[]{:S(2)}) copy-start(f32[512]{0:T(512)} %param.7) | copy-start | bytes 6148
  7.2 13.1 %copy-start.3 = (bf16[512,2,256]{2,1,0:T(2,128)(2,1)S(1)}, bf16[512,2,256]{2,1,0:T(2,128)(2,1)}, u32[]{:S(2)}) copy-start(bf16[512,2,256]{2,1,0:T(2,128)(2,1)} %param.6) | copy-start | bytes 1572868
  7.2 13.1 %copy-start.4 = (bf16[512,2,256]{2,1,0:T(2,128)(2,1)S(1)}, bf16[512,2,256]{2,1,0:T(2,128)(2,1)}, u32[]{:S(2)}) copy-start(bf16[512,2,256]{2,1,0:T(2,128)(2,1)} %param.5) | copy-start | bytes 1572868
  11.3 11.2 %collective-permute-start.3 = (bf16[256,768]{1,0:T(8,128)(2,1)}, bf16[256,768]{1,0:T(8,128)(2,1)S(1)}, u32[]{:S(2)}, u32[]{:S(2)}) collective-permute-start(bf16[256,768]{1,0:T(8,128)(2,1)} %get-tuple-element.18), channel_id=1, source_target_pairs={{0,128},{32,160},{64,192},{96,224},{128,0},{160,32},{192,64},{224,... | collective-permute-start | bytes 1179656 | tf_op jit(solution)/shard_map/ppermute | solution.py:161
  12.9 13.9 %collective-permute-start.4 = (bf16[256,768]{1,0:T(8,128)(2,1)}, bf16[256,768]{1,0:T(8,128)(2,1)S(1)}, u32[]{:S(2)}, u32[]{:S(2)}) collective-permute-start(bf16[256,768]{1,0:T(8,128)(2,1)} %get-tuple-element.19), channel_id=1, source_target_pairs={{0,64},{32,96},{64,0},{96,32},{128,192},{160,224},{192,128},{224,1... | collective-permute-start | bytes 1179656 | tf_op jit(solution)/shard_map/ppermute | solution.py:161
  15.1 20.0 %collective-permute-start.5 = (bf16[256,768]{1,0:T(8,128)(2,1)}, bf16[256,768]{1,0:T(8,128)(2,1)S(1)}, u32[]{:S(2)}, u32[]{:S(2)}) collective-permute-start(bf16[256,768]{1,0:T(8,128)(2,1)} %get-tuple-element.20), channel_id=1, source_target_pairs={{0,192},{32,224},{64,128},{96,160},{128,64},{160,96},{192,0},{224,... | collective-permute-start | bytes 1179656 | tf_op jit(solution)/shard_map/ppermute | solution.py:161
  16.4 27.3 %collective-permute-start.6 = (bf16[256,768]{1,0:T(8,128)(2,1)}, bf16[256,768]{1,0:T(8,128)(2,1)S(1)}, u32[]{:S(2)}, u32[]{:S(2)}) collective-permute-start(bf16[256,768]{1,0:T(8,128)(2,1)} %get-tuple-element.21), channel_id=1, source_target_pairs={{0,32},{32,64},{64,96},{96,0},{128,160},{160,192},{192,224},{224,1... | collective-permute-start | bytes 1179656 | tf_op jit(solution)/shard_map/ppermute | solution.py:161
  17.9 34.3 %collective-permute-start.7 = (bf16[256,768]{1,0:T(8,128)(2,1)}, bf16[256,768]{1,0:T(8,128)(2,1)}, u32[]{:S(2)}, u32[]{:S(2)}) collective-permute-start(bf16[256,768]{1,0:T(8,128)(2,1)} %get-tuple-element.22), channel_id=1, source_target_pairs={{0,160},{32,192},{64,224},{96,128},{128,32},{160,64},{192,96},{224... | collective-permute-start | bytes 1179656 | tf_op jit(solution)/shard_map/ppermute | solution.py:161
  20.1 3.1 %copy-start.6 = (s32[512,2]{0,1:T(2,128)S(1)}, s32[512,2]{0,1:T(2,128)}, u32[]{:S(2)}) copy-start(s32[512,2]{0,1:T(2,128)} %param.8) | copy-start | bytes 12292
  20.3 2.2 %copy-start.13 = (bf16[256,768]{1,0:T(8,128)(2,1)S(1)}, bf16[256,768]{1,0:T(8,128)(2,1)}, u32[]{:S(2)}) copy-start(bf16[256,768]{1,0:T(8,128)(2,1)} %get-tuple-element.23) | copy-start | bytes 1179652
  22.4 53.6 %copy-start.9 = (bf16[256,768]{1,0:T(8,128)(2,1)}, bf16[256,768]{1,0:T(8,128)(2,1)S(1)}, u32[]{:S(2)}) copy-start(bf16[256,768]{1,0:T(8,128)(2,1)S(1)} %collective-permute-done.3.refs_6_) | copy-start | bytes 1179652
  22.4 31.0 %collective-permute-start.8 = (bf16[256,768]{1,0:T(8,128)(2,1)S(1)}, bf16[256,768]{1,0:T(8,128)(2,1)}, u32[]{:S(2)}, u32[]{:S(2)}) collective-permute-start(bf16[256,768]{1,0:T(8,128)(2,1)S(1)} %copy-done.13), channel_id=1, source_target_pairs={{0,96},{32,0},{64,32},{96,64},{128,224},{160,128},{192,160},{224,1... | collective-permute-start | bytes 1179656 | tf_op jit(solution)/shard_map/ppermute | solution.py:161
  23.3 52.8 %copy-start.2 = (bf16[528,512]{1,0:T(8,128)(2,1)}, bf16[528,512]{1,0:T(8,128)(2,1)S(1)}, u32[]{:S(2)}) copy-start(bf16[528,512]{1,0:T(8,128)(2,1)S(1)} %fusion.6.refs_1_) | copy-start | bytes 1622020
  26.8 49.3 %copy-start.10 = (bf16[256,768]{1,0:T(8,128)(2,1)}, bf16[256,768]{1,0:T(8,128)(2,1)S(1)}, u32[]{:S(2)}) copy-start(bf16[256,768]{1,0:T(8,128)(2,1)S(1)} %collective-permute-done.4.refs_7_) | copy-start | bytes 1179652
  26.8 29.1 %collective-permute-start = (bf16[528,512]{1,0:T(8,128)(2,1)S(1)}, bf16[528,512]{1,0:T(8,128)(2,1)}, u32[]{:S(2)}, u32[]{:S(2)}) collective-permute-start(bf16[528,512]{1,0:T(8,128)(2,1)S(1)} %fusion.6.refs_1_), channel_id=1, source_target_pairs={{0,128},{128,0},{1,129},{129,1},{2,130},{130,2},{3,131},{131,3},{4... | collective-permute-start | bytes 1622024 | tf_op jit(solution)/shard_map/ppermute | solution.py:127
  35.1 41.0 %copy-start.11 = (bf16[256,768]{1,0:T(8,128)(2,1)}, bf16[256,768]{1,0:T(8,128)(2,1)S(1)}, u32[]{:S(2)}) copy-start(bf16[256,768]{1,0:T(8,128)(2,1)S(1)} %collective-permute-done.5.refs_8_) | copy-start | bytes 1179652
  35.1 39.3 %collective-permute-start.13 = (bf16[528,512]{1,0:T(8,128)(2,1)S(1)}, bf16[528,512]{1,0:T(8,128)(2,1)}, u32[]{:S(2)}, u32[]{:S(2)}) collective-permute-start(bf16[528,512]{1,0:T(8,128)(2,1)S(1)} %fusion.6.refs_1_), channel_id=1, source_target_pairs={{0,64},{32,96},{64,0},{96,32},{1,65},{33,97},{65,1},{97,33},{2,66}... | collective-permute-start | bytes 1622024 | tf_op jit(solution)/shard_map/ppermute | solution.py:127
  43.7 32.4 %copy-start.12 = (bf16[256,768]{1,0:T(8,128)(2,1)}, bf16[256,768]{1,0:T(8,128)(2,1)S(1)}, u32[]{:S(2)}) copy-start(bf16[256,768]{1,0:T(8,128)(2,1)S(1)} %collective-permute-done.6.refs_9_) | copy-start | bytes 1179652
  43.7 32.3 %collective-permute-start.1 = (bf16[528,512]{1,0:T(8,128)(2,1)S(1)}, bf16[528,512]{1,0:T(8,128)(2,1)S(1)}, u32[]{:S(2)}, u32[]{:S(2)}) collective-permute-start(bf16[528,512]{1,0:T(8,128)(2,1)S(1)} %fusion.6.refs_1_), channel_id=1, source_target_pairs={{0,96},{32,0},{64,32},{96,64},{1,97},{33,1},{65,33},{97,65},{2,98}... | collective-permute-start | bytes 1622024 | tf_op jit(solution)/shard_map/ppermute | solution.py:127
  52.1 23.9 %collective-permute-start.2 = (bf16[528,512]{1,0:T(8,128)(2,1)S(1)}, bf16[528,512]{1,0:T(8,128)(2,1)S(1)}, u32[]{:S(2)}, u32[]{:S(2)}) collective-permute-start(bf16[528,512]{1,0:T(8,128)(2,1)S(1)} %fusion.6.refs_1_), channel_id=1, source_target_pairs={{0,32},{32,64},{64,96},{96,0},{1,33},{33,65},{65,97},{97,1},{2,34}... | collective-permute-start | bytes 1622024 | tf_op jit(solution)/shard_map/ppermute | solution.py:127
  53.4 20.4 %collective-permute-start.9 = (bf16[256,768]{1,0:T(8,128)(2,1)}, bf16[256,768]{1,0:T(8,128)(2,1)}, u32[]{:S(2)}, u32[]{:S(2)}) collective-permute-start(bf16[256,768]{1,0:T(8,128)(2,1)} %get-tuple-element.24), channel_id=1, source_target_pairs={{0,224},{32,128},{64,160},{96,192},{128,96},{160,0},{192,32},{224,... | collective-permute-start | bytes 1179656 | tf_op jit(solution)/shard_map/ppermute | solution.py:161
  55.9 33.4 %collective-permute-start.11 = (bf16[528,512]{1,0:T(8,128)(2,1)}, bf16[528,512]{1,0:T(8,128)(2,1)}, u32[]{:S(2)}, u32[]{:S(2)}) collective-permute-start(bf16[528,512]{1,0:T(8,128)(2,1)} %collective-permute-done.refs_2_), channel_id=1, source_target_pairs={{0,32},{32,64},{64,96},{96,0},{1,33},{33,65},{65,97},{97,1},{2,34}... | collective-permute-start | bytes 1622024 | tf_op jit(solution)/shard_map/ppermute | solution.py:127
  73.8 15.5 %collective-permute-start.12 = (bf16[528,512]{1,0:T(8,128)(2,1)}, bf16[528,512]{1,0:T(8,128)(2,1)}, u32[]{:S(2)}, u32[]{:S(2)}) collective-permute-start(bf16[528,512]{1,0:T(8,128)(2,1)} %collective-permute-done.refs_2_), channel_id=1, source_target_pairs={{0,96},{32,0},{64,32},{96,64},{1,97},{33,1},{65,33},{97,65},{2,98}... | collective-permute-start | bytes 1622024 | tf_op jit(solution)/shard_map/ppermute | solution.py:127
  74.4 14.9 %collective-permute-start.14 = (bf16[528,512]{1,0:T(8,128)(2,1)}, bf16[528,512]{1,0:T(8,128)(2,1)}, u32[]{:S(2)}, u32[]{:S(2)}) collective-permute-start(bf16[528,512]{1,0:T(8,128)(2,1)} %collective-permute-done.13.refs_4_), channel_id=1, source_target_pairs={{0,128},{128,0},{1,129},{129,1},{2,130},{130,2},{3,131},{131,3},{4... | collective-permute-start | bytes 1622024 | tf_op jit(solution)/shard_map/ppermute | solution.py:127
  76.0 0.8 copy-start.7
  76.0 1.0 copy-start.8
  89.0 13.0 %collective-permute-start.10 = (bf16[16,4,16,768]{3,2,1,0:T(8,128)(2,1)}, bf16[16,4,16,768]{3,2,1,0:T(8,128)(2,1)}, u32[]{:S(2)}, u32[]{:S(2)}) collective-permute-start(bf16[16,4,16,768]{3,2,1,0:T(8,128)(2,1)} %get-tuple-element.26), channel_id=1, source_target_pairs={{0,1},{1,0},{2,3},{3,2},{4,5},{5,4},{6,7},{7,6},{8,9},{9,8},{10,11... | collective-permute-start | bytes 4718600 | tf_op jit(solution)/shard_map/ppermute | solution.py:167
  89.3 12.7 %copy-start = (bf16[16,4,16,768]{3,2,1,0:T(8,128)(2,1)S(1)}, bf16[16,4,16,768]{3,2,1,0:T(8,128)(2,1)}, u32[]{:S(2)}) copy-start(bf16[16,4,16,768]{3,2,1,0:T(8,128)(2,1)} %get-tuple-element.25) | copy-start | bytes 4718596
  101.4 3.8 %collective-permute-start.15 = (bf16[16,4,16,768]{3,2,1,0:T(8,128)(2,1)}, bf16[16,4,16,768]{3,2,1,0:T(8,128)(2,1)S(1)}, u32[]{:S(2)}, u32[]{:S(2)}) collective-permute-start(bf16[16,4,16,768]{3,2,1,0:T(8,128)(2,1)} %get-tuple-element.28), channel_id=1, source_target_pairs={{0,1},{1,0},{2,3},{3,2},{4,5},{5,4},{6,7},{7,6},{8,9},{9,8},{10,11... | collective-permute-start | bytes 4718600 | tf_op jit(solution)/shard_map/ppermute | solution.py:167
  105.1 1.4 copy-start.1
  106.6 11.0 %collective-permute-start.16 = (bf16[2,4,16,768]{3,2,1,0:T(8,128)(2,1)S(1)}, bf16[2,4,16,768]{3,2,1,0:T(8,128)(2,1)S(1)}, u32[]{:S(2)}, u32[]{:S(2)}) collective-permute-start(bf16[2,4,16,768]{3,2,1,0:T(8,128)(2,1)S(1)} %add_convert_fusion.9), channel_id=1, source_target_pairs={{0,4},{4,8},{8,12},{12,16},{16,20},{20,24},{24,28},{28,0},{1,5},{5... | collective-permute-start | bytes 589832 | tf_op jit(solution)/shard_map/ppermute | solution.py:127
  117.7 11.6 %collective-permute-start.17 = (bf16[2,4,16,768]{3,2,1,0:T(8,128)(2,1)S(1)}, bf16[2,4,16,768]{3,2,1,0:T(8,128)(2,1)S(1)}, u32[]{:S(2)}, u32[]{:S(2)}) collective-permute-start(bf16[2,4,16,768]{3,2,1,0:T(8,128)(2,1)S(1)} %get-tuple-element.33), channel_id=1, source_target_pairs={{0,4},{4,8},{8,12},{12,16},{16,20},{20,24},{24,28},{28,0},{1,5},{5... | collective-permute-start | bytes 589832 | tf_op jit(solution)/shard_map/ppermute | solution.py:127
  117.8 11.5 %collective-permute-start.20 = (bf16[2,4,16,768]{3,2,1,0:T(8,128)(2,1)S(1)}, bf16[2,4,16,768]{3,2,1,0:T(8,128)(2,1)S(1)}, u32[]{:S(2)}, u32[]{:S(2)}) collective-permute-start(bf16[2,4,16,768]{3,2,1,0:T(8,128)(2,1)S(1)} %get-tuple-element.34), channel_id=1, source_target_pairs={{0,28},{4,0},{8,4},{12,8},{16,12},{20,16},{24,20},{28,24},{1,29},{... | collective-permute-start | bytes 589832 | tf_op jit(solution)/shard_map/ppermute | solution.py:127
  129.4 9.9 %collective-permute-start.18 = (bf16[2,4,16,768]{3,2,1,0:T(8,128)(2,1)S(1)}, bf16[2,4,16,768]{3,2,1,0:T(8,128)(2,1)S(1)}, u32[]{:S(2)}, u32[]{:S(2)}) collective-permute-start(bf16[2,4,16,768]{3,2,1,0:T(8,128)(2,1)S(1)} %get-tuple-element.31), channel_id=1, source_target_pairs={{0,4},{4,8},{8,12},{12,16},{16,20},{20,24},{24,28},{28,0},{1,5},{5... | collective-permute-start | bytes 589832 | tf_op jit(solution)/shard_map/ppermute | solution.py:127
  129.5 9.8 %collective-permute-start.21 = (bf16[2,4,16,768]{3,2,1,0:T(8,128)(2,1)S(1)}, bf16[2,4,16,768]{3,2,1,0:T(8,128)(2,1)S(1)}, u32[]{:S(2)}, u32[]{:S(2)}) collective-permute-start(bf16[2,4,16,768]{3,2,1,0:T(8,128)(2,1)S(1)} %get-tuple-element.32), channel_id=1, source_target_pairs={{0,28},{4,0},{8,4},{12,8},{16,12},{20,16},{24,20},{28,24},{1,29},{... | collective-permute-start | bytes 589832 | tf_op jit(solution)/shard_map/ppermute | solution.py:127
  139.5 9.5 %collective-permute-start.22 = (bf16[2,4,16,768]{3,2,1,0:T(8,128)(2,1)S(1)}, bf16[2,4,16,768]{3,2,1,0:T(8,128)(2,1)}, u32[]{:S(2)}, u32[]{:S(2)}) collective-permute-start(bf16[2,4,16,768]{3,2,1,0:T(8,128)(2,1)S(1)} %get-tuple-element.30), channel_id=1, source_target_pairs={{0,28},{4,0},{8,4},{12,8},{16,12},{20,16},{24,20},{28,24},{1,29},{... | collective-permute-start | bytes 589832 | tf_op jit(solution)/shard_map/ppermute | solution.py:127
  143.2 7.7 %collective-permute-start.19 = (bf16[2,4,16,768]{3,2,1,0:T(8,128)(2,1)S(1)}, bf16[2,4,16,768]{3,2,1,0:T(8,128)(2,1)}, u32[]{:S(2)}, u32[]{:S(2)}) collective-permute-start(bf16[2,4,16,768]{3,2,1,0:T(8,128)(2,1)S(1)} %get-tuple-element.29), channel_id=1, source_target_pairs={{0,4},{4,8},{8,12},{12,16},{16,20},{20,24},{24,28},{28,0},{1,5},{5... | collective-permute-start | bytes 589832 | tf_op jit(solution)/shard_map/ppermute | solution.py:127
Sparse Core Ops, SparseCore 0:
  105.2 45.6 reduce-scatter.1
